TPU v7x, 256 devices: a whole 4x4x8 slice. The times are simulated.
256 devices in a mesh: frame: 64 (over x, z_lo, y), head: 4 (over z_hi, core).
Axes of the slice: x: 4, y: 4, z: 8 (z_hi: 2, z_lo: 4; z = z_hi * 4 + z_lo), core: 2. Of those that a mesh axis runs over, the one named last changes fastest.
Arguments:
- tokens_in: bfloat16 [32768, 1152], P(('frame', 'head')), may hold values from -8 to 8
- mod_shift: float32 [1152], replicated, may hold values from -3 to 3
- mod_scale: float32 [1152], replicated, may hold values from -3 to 3
- branch_gate: float32 [1152], replicated, may hold values from -4 to 4
- inproj: bfloat16 [1152, 3, 1152], P(None, None, 'head'), may hold values from -0.3 to 0.3
- outproj: bfloat16 [1152, 1152], P('head'), may hold values from -0.1875 to 0.1875
- norm_gain: float32 [2, 72], replicated, may hold values from 0.5 to 6
- grad_result: bfloat16 [32768, 1152], P(('frame', 'head')), may hold values from -24 to 24
Outputs:
- result: bfloat16 [32768, 1152], P(('frame', 'head'))
- grad_in: bfloat16 [32768, 1152], P(('frame', 'head'))
- grad_inproj: float32 [1152, 3, 1152], P('frame', None, 'head')
- grad_outproj: float32 [1152, 1152], P('head', 'frame')
All inputs are finite; a program needn't handle non-finite values.
Results may differ from a plain program's by a relative error of at most 0.024.
The roundings to bfloat16 on the way count: a program that leaves them out, or rounds other values in their place, can miss the bound.
Values may be sent and summed in bfloat16 or wider, within the bound.
A program may use at most 64 MiB of HBM per device.

v0:
```python
import jax
import jax.numpy as jnp
from jax import lax
from jax.sharding import PartitionSpec as P

HD = 72
FRAMES = 64
PIX = 512


def layer_modulate(field, mod_shift, mod_scale):
    mean = jnp.mean(field, axis=-1, keepdims=True)
    centred = field - mean
    spread = jnp.mean(centred * centred, axis=-1, keepdims=True)
    return centred * lax.rsqrt(spread + 1e-06) * (1.0 + mod_scale) + mod_shift


def qk_norm(projected, norm_gain):
    rows = projected.shape[0]
    width = projected.shape[2]
    split = projected.reshape(rows, 3, width // HD, HD)
    query = split[:, 0]
    key_part = split[:, 1]
    query = (
        query * lax.rsqrt(jnp.mean(query * query, axis=-1, keepdims=True) + 1e-06) * norm_gain[0]
    )
    key_part = (
        key_part
        * lax.rsqrt(jnp.mean(key_part * key_part, axis=-1, keepdims=True) + 1e-06)
        * norm_gain[1]
    )
    joined = jnp.stack([query, key_part, split[:, 2]], axis=1)
    return joined.reshape(rows, 3, width).astype(jnp.bfloat16)


def attend(pixel_heads):
    frames, pixels, three, width = pixel_heads.shape
    split = pixel_heads.reshape(frames, pixels, 3, width // HD, HD).astype(jnp.float32)
    query = split[:, :, 0]
    key_part = split[:, :, 1]
    value = split[:, :, 2]
    scores = jnp.einsum("fphd,gphd->phfg", query, key_part) / jnp.sqrt(jnp.float32(HD))
    peak = jnp.max(scores, axis=-1, keepdims=True)
    weights = jnp.exp(scores - peak)
    probs = (weights / jnp.sum(weights, axis=-1, keepdims=True)).astype(jnp.bfloat16)
    mixed = jnp.einsum("phfg,gphd->fphd", probs.astype(jnp.float32), value)
    return mixed.reshape(frames, pixels, width).astype(jnp.bfloat16)


def body(tokens_in, mod_shift, mod_scale, branch_gate, inproj, outproj, norm_gain, grad_result):
    frame_count = lax.axis_size("frame")
    gathered = lax.all_gather(tokens_in, "head", axis=0, tiled=True)
    rows_all = gathered.shape[0]
    frames_here = rows_all // PIX
    pixels_here = PIX // frame_count
    width = outproj.shape[0]
    modulated = layer_modulate(gathered.astype(jnp.float32), mod_shift, mod_scale).astype(
        jnp.bfloat16
    )
    in_matrix = inproj.reshape(inproj.shape[0], 3 * width)
    projected = jnp.dot(modulated, in_matrix, preferred_element_type=jnp.float32).reshape(
        rows_all, 3, width
    )
    normed = qk_norm(projected, norm_gain)
    split_rows = normed.reshape(frames_here, frame_count, pixels_here, 3, width)
    moved_heads = lax.all_to_all(split_rows, "frame", split_axis=1, concat_axis=0, tiled=True)
    pixel_heads = moved_heads.reshape(FRAMES, pixels_here, 3, width)
    mixed = attend(pixel_heads).reshape(FRAMES, 1, pixels_here, width)
    attended = lax.all_to_all(mixed, "frame", split_axis=0, concat_axis=1, tiled=True).reshape(
        rows_all, width
    )
    block = attended
    attn_out = lax.psum_scatter(
        jnp.dot(block, outproj, preferred_element_type=jnp.float32).astype(jnp.bfloat16),
        "head",
        scatter_dimension=0,
        tiled=True,
    ).astype(jnp.float32)
    result = (tokens_in.astype(jnp.float32) + branch_gate * attn_out).astype(jnp.bfloat16)
    grad_scaled = (branch_gate * grad_result.astype(jnp.float32)).astype(jnp.bfloat16)
    grad_all = lax.all_gather(grad_scaled, "head", axis=0, tiled=True)
    out_grad_turned = jnp.dot(grad_all.T, attended, preferred_element_type=jnp.float32)
    grad_outproj = lax.psum_scatter(out_grad_turned, "frame", scatter_dimension=0, tiled=True).T
    grad_attended = jnp.dot(grad_all, outproj.T, preferred_element_type=jnp.float32).astype(
        jnp.bfloat16
    )
    sent_grads = grad_attended.reshape(frames_here, frame_count, pixels_here, width)
    pixel_grads = lax.all_to_all(
        sent_grads, "frame", split_axis=1, concat_axis=0, tiled=True
    ).reshape(FRAMES, pixels_here, width)
    unused, attend_back = jax.vjp(attend, pixel_heads)
    grad_heads = attend_back(pixel_grads)[0]
    returned = lax.all_to_all(
        grad_heads.reshape(FRAMES, 1, pixels_here, 3, width),
        "frame",
        split_axis=0,
        concat_axis=1,
        tiled=True,
    )
    returned = returned.reshape(rows_all, 3, width)
    unused, norm_back = jax.vjp(lambda field: qk_norm(field, norm_gain), projected)
    grad_projected = norm_back(returned)[0].astype(jnp.bfloat16)
    grad_flat = grad_projected.reshape(rows_all, 3 * width)
    in_grad = jnp.dot(modulated.T, grad_flat, preferred_element_type=jnp.float32)
    summed_in = lax.psum_scatter(in_grad, "frame", scatter_dimension=0, tiled=True)
    grad_inproj = summed_in.reshape(summed_in.shape[0], 3, width)
    block = grad_flat
    grad_mod = lax.psum_scatter(
        jnp.dot(block, in_matrix.T, preferred_element_type=jnp.float32).astype(jnp.bfloat16),
        "head",
        scatter_dimension=0,
        tiled=True,
    ).astype(jnp.float32)
    unused, layer_back = jax.vjp(
        lambda field: layer_modulate(field, mod_shift, mod_scale), tokens_in.astype(jnp.float32)
    )
    grad_layer = layer_back(grad_mod)[0]
    grad_in = (grad_result.astype(jnp.float32) + grad_layer).astype(jnp.bfloat16)
    return (result, grad_in, grad_inproj, grad_outproj)


def solution(mesh):
    placed = (
        P(("frame", "head"), None),
        P(),
        P(),
        P(),
        P(None, None, "head"),
        P("head", None),
        P(),
        P(("frame", "head"), None),
    )
    return jax.shard_map(
        body,
        mesh=mesh,
        in_specs=placed,
        out_specs=(
            P(("frame", "head"), None),
            P(("frame", "head"), None),
            P("frame", None, "head"),
            P("head", "frame"),
        ),
        check_vma=False,
    )
```

profile of v0, /device:TPU:64, one launch (start us, length us, event | category | flops | bytes accessed | tf_op | source)
XLA Modules:
  0.0 1024.3 jit_solution(6241211419080735263)
XLA Ops:
  7.2 0.7 all-gather.3.cloned.1.call-update
  8.0 1.7 fusion.18
  9.7 0.7 broadcast_add_fusion
  10.4 0.8 slice_bitcast_fusion.1
  11.2 31.8 %all-gather.3.cloned.1.call-done = bf16[512,1152]{1,0:T(8,128)(2,1)} async-done(((bf16[128,1152]{1,0:T(8,128)(2,1)}), bf16[512,1152]{1,0:T(8,128)(2,1)}) %all-gather.3.cloned.1.call-update) | async-done | bytes 1179664 | tf_op jit(solution)/shard_map/all_gather | solution.py:52
  43.0 1.6 convert_reduce_fusion
  44.6 0.4 fusion.3
  45.1 1.5 fusion.8
  46.6 1.2 copy-done.1
  48.6 1.4 fusion.28
  50.0 24.9 %all-gather.5.cloned.1.call-done = bf16[512,1152]{1,0:T(8,128)(2,1)} async-done(((bf16[128,1152]{1,0:T(8,128)(2,1)}), bf16[512,1152]{1,0:T(8,128)(2,1)}) %all-gather.5.cloned.1.call-update) | async-done | bytes 1179664 | tf_op jit(solution)/shard_map/all_gather | solution.py:81
  74.9 2.0 convolution_convert_fusion.3
  77.0 1.0 copy.41
  77.9 10.4 %all-to-all-start.2 = ((bf16[1,64,8,288]{3,2,0,1:T(8,128)(2,1)}), bf16[1,64,8,288]{3,2,0,1:T(8,128)(2,1)}, u32[]{:S(2)}, u32[]{:S(2)}) async-start(bf16[1,64,8,288]{3,2,0,1:T(8,128)(2,1)} %bitcast.16), calls=%async_computation.3 | async-start | bytes 786432 | tf_op jit(solution)/shard_map/all_to_all | solution.py:88
  88.4 2.1 multiply_convert_fusion.1
  91.1 1.3 copy.31
  92.4 1.1 stack.11
  93.5 1.3 pad_maximum_fusion
  94.8 1.2 copy.34
  95.9 6.2 all-to-all-done.2
  102.1 7.1 all-to-all-start
  109.4 2.2 reshape.213
  111.6 26.6 %all-to-all-done = bf16[1,64,8,3,288]{4,2,3,0,1:T(8,128)(2,1)S(1)} async-done(((bf16[1,64,8,3,288]{4,2,3,0,1:T(8,128)(2,1)}), bf16[1,64,8,3,288]{4,2,3,0,1:T(8,128)(2,1)S(1)}, u32[]{:S(2)}, u32[]{:S(2)}) %all-to-all-start) | async-done | bytes 884768 | tf_op jit(solution)/shard_map/all_to_all | solution.py:66
  138.2 2.0 reshape_reshape.2
  140.2 1.9 fusion.57
  142.1 0.6 fusion.58
  142.9 0.4 copy-done.12
  143.4 0.7 fusion.13
  144.1 0.8 convert_reduce_fusion.1
  144.9 0.7 convolution_bitcast_fusion.2
  145.6 0.7 convolution_bitcast_fusion.3
  146.3 0.4 convolution_bitcast_fusion.1
  146.7 0.4 add_convert_fusion
  147.2 2.4 copy.45
  149.5 3.8 reshape.214
  153.4 36.7 %all_to_all.16 = bf16[64,1,8,3,288]{4,2,3,1,0:T(8,128)(2,1)S(1)} all-to-all(bf16[64,1,8,3,288]{4,2,3,1,0:T(8,128)(2,1)} %bitcast.126), channel_id=1, replica_groups=mesh['frame'=64,'head'=4] {'frame'}, dimensions={0} | all-to-all | bytes 1769472 | tf_op jit(solution)/shard_map/all_to_all | solution.py:93
  190.0 1.6 copy.47
  191.6 4.7 reshape.216
  196.4 3.6 fusion.56
  200.0 2.4 copy.58
  202.4 2.4 copy.59
  204.7 2.4 copy.57
  207.2 2.0 fusion.26
  209.5 1.4 add_add_fusion.2
  211.1 0.9 copy-done.10
  212.0 2.6 fusion
  214.7 1.5 fusion.7
  216.2 0.4 copy.39
  216.9 20.3 %all_to_all.17 = bf16[64,1,8,288]{3,2,1,0:T(8,128)(2,1)S(1)} all-to-all(bf16[64,1,8,288]{3,2,1,0:T(8,128)(2,1)S(1)} %bitcast.127), channel_id=1, replica_groups=mesh['frame'=64,'head'=4] {'frame'}, dimensions={0} | all-to-all | bytes 589824 | tf_op jit(solution)/shard_map/all_to_all | solution.py:69
  237.2 0.7 copy-done.7
  238.0 2.9 convolution_convert_fusion
  241.0 3.6 fusion.39
  244.6 3.6 fusion.50
  248.2 0.6 copy-done.16
  248.9 0.6 dynamic-slice
  250.2 5.0 reduce-scatter.5.cloned.1.call-done
  255.3 1.2 fusion.20
  256.5 1.3 fusion.42
  257.8 43.7 %reduce-scatter.3.cloned.1.call-done = bf16[128,1152]{1,0:T(8,128)(2,1)} async-done(((bf16[512,1152]{1,0:T(8,128)(2,1)}), bf16[128,1152]{1,0:T(8,128)(2,1)}) %reduce-scatter.3.cloned.1.call-update) | async-done | bytes 294928 | tf_op jit(solution)/shard_map/reduce_scatter | solution.py:73
  301.5 2.1 fusion.19
  303.6 711.1 %all-reduce.11.cloned.1.call-done = (f32[1152,864]{1,0:T(8,128)}, f32[1152,288]{1,0:T(8,128)}) async-done(((f32[1152,864]{1,0:T(8,128)}, f32[1152,288]{1,0:T(8,128)}), (f32[1152,864]{1,0:T(8,128)}, f32[1152,288]{1,0:T(8,128)})) %all-reduce.11.cloned.1.call-update) | async-done | bytes 5308432
  1014.7 0.9 constant_dynamic-slice_fusion
  1015.6 0.8 reshape.215
  1016.4 1.4 dynamic-slice_bitcast_fusion
  (58 shorter events, 3.1 us)
Async XLA Ops:
  7.2 37.9 %copy-start = (bf16[1152,3,288]{0,2,1:T(8,128)(2,1)S(1)}, bf16[1152,3,288]{0,2,1:T(8,128)(2,1)}, u32[]{:S(2)}) copy-start(bf16[1152,3,288]{0,2,1:T(8,128)(2,1)} %param.12) | copy-start | bytes 5971972
  7.2 37.9 %copy-start.15 = (f32[1152]{0:T(1024)S(1)}, f32[1152]{0:T(1024)}, u32[]{:S(2)}) copy-start(f32[1152]{0:T(1024)} %param.9) | copy-start | bytes 13828
  7.2 35.8 %all-gather.3.cloned.1.call-start = ((), (), s32[]{:S(2)}) async-start(), calls=%async_computation.6 | async-start | bytes 1474560 | tf_op jit(solution)/shard_map/all_gather | solution.py:52
  7.9 67.0 %all-gather.5.cloned.1.call-start = ((), (), s32[]{:S(2)}) async-start(), calls=%async_computation.8 | async-start | bytes 1474560 | tf_op jit(solution)/shard_map/all_gather | solution.py:81
  43.0 1.6 copy-start.5
  46.6 1.3 copy-start.1
  77.9 24.2 %all-to-all-start.2 = ((bf16[1,64,8,288]{3,2,0,1:T(8,128)(2,1)}), bf16[1,64,8,288]{3,2,0,1:T(8,128)(2,1)}, u32[]{:S(2)}, u32[]{:S(2)}) async-start(bf16[1,64,8,288]{3,2,0,1:T(8,128)(2,1)} %bitcast.16), calls=%async_computation.3 | async-start | bytes 786432 | tf_op jit(solution)/shard_map/all_to_all | solution.py:88
  102.1 36.1 %all-to-all-start = ((bf16[1,64,8,3,288]{4,2,3,0,1:T(8,128)(2,1)}), bf16[1,64,8,3,288]{4,2,3,0,1:T(8,128)(2,1)S(1)}, u32[]{:S(2)}, u32[]{:S(2)}) async-start(bf16[1,64,8,3,288]{4,2,3,0,1:T(8,128)(2,1)} %copy.34), calls=%async_computation | async-start | bytes 2359296 | tf_op jit(solution)/shard_map/all_to_all | solution.py:66
  109.2 146.1 %reduce-scatter.5.cloned.1.call-start = ((), (), s32[]{:S(2)}) async-start(), calls=%async_computation.9 | async-start | bytes 1474560 | tf_op jit(solution)/shard_map/reduce_scatter | solution.py:108
  142.1 1.9 copy-start.13
  142.1 1.2 copy-start.12
  207.2 2.2 copy-start.2
  207.2 2.3 copy-start.4
  209.5 1.4 copy-start.8
  211.0 0.9 copy-start.10
  214.6 86.9 %reduce-scatter.3.cloned.1.call-start = ((), (), s32[]{:S(2)}) async-start(), calls=%async_computation.7 | async-start | bytes 1474560 | tf_op jit(solution)/shard_map/reduce_scatter | solution.py:73
  237.2 0.8 copy-start.7
  240.9 3.7 copy-start.6
  240.9 773.8 %all-reduce.11.cloned.1.call-start = ((), (), s32[]{:S(2)}) async-start(), calls=%async_computation.10 | async-start | bytes 11796480
  240.9 3.6 copy-start.11
  248.2 0.7 copy-start.16
  248.2 1.9 copy-start.3
  248.2 53.3 %copy-start.9 = (bf16[128,1152]{1,0:T(8,128)(2,1)S(1)}, bf16[128,1152]{1,0:T(8,128)(2,1)}, u32[]{:S(2)}) copy-start(bf16[128,1152]{1,0:T(8,128)(2,1)} %param.15) | copy-start | bytes 884740
  248.2 53.3 %copy-start.14 = (f32[1152]{0:T(1024)S(1)}, f32[1152]{0:T(1024)}, u32[]{:S(2)}) copy-start(f32[1152]{0:T(1024)} %param.11) | copy-start | bytes 13828
Sparse Core Ops, SparseCore 0:
  9.8 33.0 all-gather.2
  45.3 29.5 all-gather.4
  214.7 40.4 reduce-scatter.4
  258.2 43.2 reduce-scatter.2
  304.1 710.5 all-reduce.10
where the time goes:
time: 1040 us; the launch traced here: 1020 us
  waiting for transfers between devices  850 us (82%)
  blocking collectives  56.9 us (5%)
  local copies, waits for them, and re-layouts  44.7 us (4%)
  matrix products  20.9 us (2%)
  other arithmetic  19 us (2%)
  starting transfers between devices  17.9 us (2%)
  between operations  14.7 us (1%)
    unnamed x6, waiting for transfers between devices  712 us
    reduce_scatter x1, waiting for transfers between devices, body(): lax.psum_scatter(jnp.dot(block, outproj, preferred_element_type=jnp.float...  43.7 us
    all_to_all x1, blocking collectives, body(): lax.all_to_all(grad_heads.reshape(FRAMES, 1, pixels_here, 3, width), 'fra...  36.7 us
    all_gather x1, waiting for transfers between devices, body(): gathered = lax.all_gather(tokens_in, 'head', axis=0, tiled=True)  31.8 us
    all_to_all x1, waiting for transfers between devices, body(): lax.all_to_all(split_rows, 'frame', split_axis=1, concat_axis=0, tiled=True)  26.6 us
    all_gather x1, waiting for transfers between devices, body(): grad_all = lax.all_gather(grad_scaled, 'head', axis=0, tiled=True)  24.9 us
  transfers between devices with their start and end apart: 7, of which 7 were waited for; matrix products, arithmetic and copies ran while one was open for 4% of the time, Pallas kernels for 0%

commit v1 on v0

v1 whole, which is shorter than its diff:
```python
import functools

import jax
import jax.numpy as jnp
import ml_dtypes
import numpy as np
from jax import lax
from jax.experimental import pallas as pl
from jax.experimental.pallas import tpu as pltpu
from jax.sharding import PartitionSpec as P

D = 1152
HD = 72
W2 = 640
HW = 384
BF = jnp.bfloat16
F32 = jnp.float32
MESH = pl.DeviceIdType.MESH

STAGE1 = [(0, dz, dh, 0, 0, 0) for dz in range(4) for dh in range(2)]
STAGE2 = [(dx, 0, 0, dl, 0, 0) for dx in range(4) for dl in range(2)]
CORE = (0, 0, 0, 0, 0, 1)
ZHI = (0, 0, 0, 0, 1, 0)
XS = [(dx, 0, 0, 0, 0, 0) for dx in (1, 2, 3)]
YS = [(0, 0, dh, dl, 0, 0) for dh, dl in ((0, 1), (1, 0), (1, 1))]
ZSAME = [(0, dz, 0, 0, 0, 0) for dz in (1, 2, 3)]
ZOTHER = [(0, dz, 0, 0, 1, 0) for dz in range(4)]
PARTNERS = []
for _off in STAGE1[1:] + STAGE2[1:] + [CORE] + XS + YS + ZSAME + ZOTHER:
    if _off not in PARTNERS:
        PARTNERS.append(_off)


def one_hot(rows, cols, source):
    made = np.zeros((rows, cols), np.float32)
    for row in range(rows):
        col = source(row)
        if col is not None:
            made[row, col] = 1.0
    return made.astype(ml_dtypes.bfloat16)


def constants():
    swap = one_hot(128, 128, lambda o: (o // 2 % 8) * 16 + (o // 16) * 2 + o % 2)
    turn = one_hot(
        D, D, lambda t: (t % 288 // 72) * 288 + (t % 72 // 18) * 72 + (t // 288) * 18 + t % 18
    )
    first = one_hot(
        320,
        288,
        lambda o: (o % 80 // 18) * 72 + (o // 80) * 18 + o % 80 % 18 if o % 80 < 72 else None,
    )
    second = one_hot(320, 288, lambda o: (o // 80) * 72 + o % 80 if o % 80 < 72 else None)
    upper = one_hot(192, 80, lambda o: (o // 48) * 18 + o % 48 if o % 48 < 18 else None)
    lower = one_hot(
        192, 80, lambda o: (o // 48) * 18 + o % 48 - 18 if 18 <= o % 48 < 36 else None
    )
    heads = np.zeros((HW, HW), np.float32)
    for h in range(4):
        heads[h * HD : (h + 1) * HD, h * HD : (h + 1) * HD] = 1.0
    return (swap, turn, first, second, upper, lower, heads.astype(ml_dtypes.bfloat16))


def mm(a, b):
    return jnp.dot(a, b, preferred_element_type=F32)


def mm_nt(a, b):
    return lax.dot_general(a, b, (((1,), (1,)), ((), ())), preferred_element_type=F32)


def mm_tn(a, b):
    return lax.dot_general(a, b, (((0,), (0,)), ((), ())), preferred_element_type=F32)


def head_sum(values, ones):
    high = values.astype(BF)
    low = (values - high.astype(F32)).astype(BF)
    return mm(high, ones) + mm(low, ones)


def kernel(
    tok, grd, shift, scale, gate, gains, wa, swap, turn_hbm, first, second, upper, lower,
    heads,
    res_out, gin_out, sum_out,
    turn, wo, r1, per, full, mod, mod_t, both_t, gs, xf, yf, xn, kn, ga, rq, rk,
    acc_o, acc_q, acc_k, acc_v, ao, gm, gx, g1, g2, s1, s2, q1, zb, zr, cs, cr, ob, back, backp, fin,
    local_sem, ssem, rsem,
):
    f = lax.axis_index("frame")
    h = lax.axis_index("head")
    x, z, yh, yl = f // 16, (f // 4) % 4, (f // 2) % 2, f % 2
    zh, c = h // 2, h % 2
    y = yh * 2 + yl

    def coords(off):
        return (
            (x + off[0]) % 4,
            (z + off[1]) % 4,
            (yh + off[2]) % 2,
            (yl + off[3]) % 2,
            (zh + off[4]) % 2,
            (c + off[5]) % 2,
        )

    def dev(off):
        px, pz, ph, pw, pzh, pc = coords(off)
        return ((px * 4 + pz) * 4 + ph * 2 + pw, pzh * 2 + pc)

    count = [0]
    started = []

    def send(src, dst, off):
        at = count[0]
        count[0] += 1
        copy = pltpu.make_async_remote_copy(
            src_ref=src, dst_ref=dst, send_sem=ssem.at[at], recv_sem=rsem.at[at],
            device_id=dev(off), device_id_type=MESH,
        )
        copy.start()
        started.append(copy)
        return copy

    def rows(start, size):
        return pl.ds(pl.multiple_of(start, 16), size)

    load_turn = pltpu.make_async_copy(turn_hbm, turn, local_sem.at[0])
    load_turn.start()

    barrier = pltpu.get_barrier_semaphore()
    for off in PARTNERS:
        pl.semaphore_signal(barrier, inc=1, device_id=dev(off), device_id_type=MESH)
    pl.semaphore_wait(barrier, len(PARTNERS))

    def piece(px, py):
        return py % 2, (px * 2 + py // 2) * 144

    part, start = piece(x, y)
    w_z = send(wa.at[part, rows(start, 144)], wo.at[part, rows(start, 144)], ZHI)

    def stage1(src, which):
        out = []
        for slot, off in enumerate(STAGE1):
            _, pz, ph, _, _, _ = coords(off)
            block = rows((pz * 2 + ph) * 16, 16)
            if slot == 0:
                r1[which, 0:16, :] = src[block, :]
            else:
                out.append(send(src.at[block], r1.at[which, pl.ds(slot * 16, 16)], off))
        return out

    def stage2(which):
        per[which] = mm(swap[...], r1[which]).astype(BF)
        out = []
        for slot, off in enumerate(STAGE2):
            px, _, _, pw, _, _ = coords(off)
            block = rows((px * 2 + pw) * 16, 16)
            if slot == 0:
                full[which, 0:16, :] = per[which, block, :]
            else:
                out.append(
                    send(per.at[which, block], full.at[which, pl.ds(slot * 16, 16)], off)
                )
        return out

    def to_core(which):
        return send(full.at[which, pl.ds(0, 128)], full.at[which, pl.ds(128, 128)], CORE)

    def arrived(copies):
        for copy in copies:
            copy.wait_recv()

    tok1 = stage1(tok, 0)
    grd1 = stage1(grd, 1)

    w_z.wait_recv()
    w_x1 = [send(wo.at[part, rows(start, 80)], wo.at[part, rows(start, 80)], off) for off in XS]
    w_y1 = [
        send(wo.at[part, rows(start + 80, 64)], wo.at[part, rows(start + 80, 64)], off)
        for off in YS
    ]
    w_last = [send(wo.at[part, rows(start, 80)], wo.at[part, rows(start, 80)], off) for off in YS]
    w_last += [
        send(wo.at[part, rows(start + 80, 64)], wo.at[part, rows(start + 80, 64)], off)
        for off in XS
    ]

    arrived(tok1)
    tok2 = stage2(0)

    for copy, off in zip(w_x1, XS):
        copy.wait_recv()
        p2, st2 = piece((x - off[0]) % 4, y)
        w_last += [
            send(wo.at[p2, rows(st2, 80)], wo.at[p2, rows(st2, 80)], other) for other in YS
        ]
    for copy, off in zip(w_y1, YS):
        copy.wait_recv()
        p2, st2 = piece(x, ((yh + off[2]) % 2) * 2 + (yl + off[3]) % 2)
        w_last += [
            send(wo.at[p2, rows(st2 + 80, 64)], wo.at[p2, rows(st2 + 80, 64)], other)
            for other in XS
        ]

    arrived(tok2)
    tok3 = to_core(0)
    arrived(grd1)
    grd2 = stage2(1)
    load_turn.wait()
    tok3.wait_recv()

    def modulate(i, carry):
        at = pl.ds(pl.multiple_of(i * 32, 32), 32)
        field = full[0, at, :].astype(F32)
        mean = jnp.mean(field, axis=-1, keepdims=True)
        centred = field - mean
        spread = jnp.mean(centred * centred, axis=-1, keepdims=True)
        mod[at, :] = (
            centred * lax.rsqrt(spread + 1e-06) * (1.0 + scale[...]) + shift[...]
        ).astype(BF)
        return carry

    lax.fori_loop(0, 8, modulate, 0)
    mod_t[...] = mod[...].T
    both_t[:, 0:256] = mm(turn[...], mod_t[...]).astype(BF)

    lane = lax.broadcasted_iota(jnp.int32, (1, HW), 1)
    row_i = lax.broadcasted_iota(jnp.int32, (256, 256), 0)
    col_i = lax.broadcasted_iota(jnp.int32, (256, 256), 1)
    gain_q = gains[0:1, :]
    gain_k = gains[1:2, :]

    def forward(w):
        xf[...] = mm(mod[...], w[0])
        yf[...] = mm(mod[...], w[1, :, 0:HW])
        q = xf[:, 0:HW]
        q = jnp.where(lane < 288, q, 0.0)
        r = lax.rsqrt(head_sum(q * q, heads[...]) * (1.0 / HD) + 1e-06)
        rq[...] = r
        qn = jnp.where(lane < 288, q * r * gain_q, xf[:, 0:HW])
        xn[:, 0:HW] = qn.astype(BF)
        xn[:, HW:W2] = xf[:, HW:W2].astype(BF)
        k = jnp.where(lane < 288, yf[...], 0.0)
        r = lax.rsqrt(head_sum(k * k, heads[...]) * (1.0 / HD) + 1e-06)
        rk[...] = r
        kn[...] = (k * r * gain_k).astype(BF)

    def attention():
        acc_o[...] = jnp.zeros_like(acc_o)
        acc_q[...] = jnp.zeros_like(acc_q)
        acc_k[...] = jnp.zeros_like(acc_k)
        acc_v[...] = jnp.zeros_like(acc_v)
        same = (row_i // 128 == col_i // 128) & (row_i % 2 == col_i % 2)
        root = 1.0 / np.sqrt(np.float32(HD))

        def head(i, carry):
            in_q = (lane >= i * HD) & (lane < i * HD + HD)
            in_v = (lane >= i * HD + 32) & (lane < i * HD + 32 + HD)
            zero = jnp.zeros((), BF)
            qh = jnp.where(in_q, xn[:, 0:HW], zero)
            kh = jnp.where(in_q, kn[...], zero)
            vh = jnp.where(in_v, xn[:, 256:W2], zero)
            gh = jnp.where(in_v, ga[...], zero)
            s = jnp.where(same, mm_nt(qh, kh) * root, -1e30)
            e = jnp.exp(s - jnp.max(s, axis=-1, keepdims=True))
            p = e * (1.0 / jnp.sum(e, axis=-1, keepdims=True))
            pb = p.astype(BF)
            acc_o[...] += mm(pb, vh)
            acc_v[...] += mm_tn(pb, gh)
            dp = mm_nt(gh, vh)
            ds = (p * (dp - jnp.sum(p * dp, axis=-1, keepdims=True)) * root).astype(BF)
            acc_q[...] += mm(ds, kh)
            acc_k[...] += mm_tn(ds, qh)
            return carry

        lax.fori_loop(0, 4, head, 0)

    def unnorm(cot, raw, r, gain):
        n = jnp.where(lane < 288, raw * r, 0.0)
        dn = cot.astype(BF).astype(F32) * gain
        inner = head_sum(n * dn, heads[...]) * (1.0 / HD)
        return jnp.where(lane < 288, r * (dn - n * inner), 0.0).astype(BF)

    def backward(g, w):
        gq = unnorm(acc_q[...], xf[:, 0:HW], rq[...], gain_q)
        gk = unnorm(acc_k[...], yf[...], rk[...], gain_k)
        gv = acc_v[...].astype(BF)
        att = acc_o[...].astype(BF)
        gx[0:256, 0:256] = gq[:, 0:256]
        gx[0:256, 256:HW] = gq[:, 256:HW] + gv[:, 0:128]
        gx[0:256, HW:W2] = gv[:, 128:HW]
        gx[256:512, 0:HW] = gk
        gx[256:512, HW:W2] = jnp.zeros((256, W2 - HW), BF)
        gx[512:768, 0:256] = jnp.zeros((256, 256), BF)
        gx[512:768, 256:W2] = att

        def grads(i, carry):
            at = pl.ds(pl.multiple_of(i * 288, 288), 288)
            g1[g, at, :] = mm(mod_t[at, :], gx[0:256, :]).astype(BF)
            g2[g, at, :] = mm(both_t[at, :], gx[256:768, :]).astype(BF)
            return carry

        lax.fori_loop(0, 4, grads, 0)
        out = mm_nt(gx[512:768, 256:W2], w[1, :, 256:W2])
        back_mod = mm_nt(gx[0:256, :], w[0]) + mm_nt(gx[256:512, 0:HW], w[1, :, 0:HW])
        if g == 0:
            ao[...] = out
            gm[...] = back_mod
        else:
            ao[...] += out
            gm[...] += back_mod

    def reduce_first(g):
        a, b = [], []
        for i, off in enumerate(XS):
            px = coords(off)[0]
            a.append(send(g1.at[g, rows(px * 288, 288)], s1.at[g, 0, i], off))
        for i, off in enumerate(YS):
            _, _, ph, pw, _, _ = coords(off)
            b.append(send(g2.at[g, rows((ph * 2 + pw) * 288, 288)], s1.at[g, 1, i], off))
        return a, b

    def reduce_second(g, copies):
        out = []
        for half, (grad, at, spread, offs) in enumerate(
            ((g1, x, first, YS), (g2, y, second, XS))
        ):
            arrived(copies[half])
            total = grad[g, rows(at * 288, 288), :].astype(F32)
            for i in range(3):
                total = total + s1[g, half, i].astype(F32)
            q1[g, half] = mm(spread[...], total.astype(BF)).astype(BF)
            sent = []
            for i, off in enumerate(offs):
                px, _, ph, pw, _, _ = coords(off)
                to = ph * 2 + pw if half == 0 else px
                sent.append(send(q1.at[g, half, rows(to * 80, 80)], s2.at[g, half, i], off))
            out.append(sent)
        return out

    def reduce_z(g, copies):
        sums = []
        for half, at in ((0, y), (1, x)):
            arrived(copies[half])
            total = q1[g, half, rows(at * 80, 80), :].astype(F32)
            for i in range(3):
                total = total + s2[g, half, i].astype(F32)
            sums.append(total.astype(BF))
        zb[g] = (mm(upper[...], sums[0]) + mm(lower[...], sums[1])).astype(BF)
        out = []
        for off in ZSAME if g == 0 else ZOTHER:
            slot = off[1] - 1 if g == 0 else 3 + off[1]
            pz = coords(off)[1]
            out.append(send(zb.at[g, rows(pz * 48, 48)], zr.at[slot], off))
        return out

    forward(wa)
    arrived(grd2)
    grd3 = to_core(1)
    grd3.wait_recv()
    gs[...] = (full[1].astype(F32) * gate[...]).astype(BF)
    mod_t2 = gs[...].T
    both_t[:, 256:512] = mm(turn[...], mod_t2).astype(BF)

    def cotangent(w):
        raw = mm(gs[...], w[1, :, 256:W2])
        ga[...] = jnp.where((lane >= 32) & (lane < 320), raw, 0.0).astype(BF)

    cotangent(wa)
    attention()
    backward(0, wa)
    sum_a = reduce_first(0)
    arrived(w_last)
    forward(wo)
    cotangent(wo)
    attention()
    backward(1, wo)
    sum_b = reduce_first(1)

    cs[0] = ao[128:256, :].astype(BF)
    cs[1] = gm[128:256, :].astype(BF)
    shares = [send(cs.at[i], cr.at[i], CORE) for i in range(2)]

    def back_stage2(which):
        out = []
        for slot, off in enumerate(STAGE2):
            inv = tuple(-v for v in off)
            block = rows((x * 2 + yl) * 16, 16)
            if slot == 0:
                back[which, block, :] = ob[which, 0:16, :]
            else:
                out.append(send(ob.at[which, pl.ds(slot * 16, 16)], back.at[which, block], inv))
        return out

    def back_stage1(which):
        backp[which] = mm(swap[...], back[which]).astype(BF)
        out = []
        for slot, off in enumerate(STAGE1):
            inv = tuple(-v for v in off)
            block = rows((z * 2 + yh) * 16, 16)
            if slot == 0:
                fin[which, block, :] = backp[which, 0:16, :]
            else:
                out.append(send(backp.at[which, pl.ds(slot * 16, 16)], fin.at[which, block], inv))
        return out

    shares[0].wait_recv()
    ob[0] = (
        full[0, 0:128, :].astype(F32) + gate[...] * (ao[0:128, :] + cr[0].astype(F32))
    ).astype(BF)
    res2 = back_stage2(0)
    shares[1].wait_recv()

    def layer_back(i, carry):
        at = pl.ds(pl.multiple_of(i * 32, 32), 32)
        field = full[0, at, :].astype(F32)
        mean = jnp.mean(field, axis=-1, keepdims=True)
        centred = field - mean
        spread = jnp.mean(centred * centred, axis=-1, keepdims=True)
        r = lax.rsqrt(spread + 1e-06)
        hat = centred * r
        d = (gm[at, :] + cr[1, at, :].astype(F32)) * (1.0 + scale[...])
        dx = r * (
            d
            - jnp.mean(d, axis=-1, keepdims=True)
            - hat * jnp.mean(d * hat, axis=-1, keepdims=True)
        )
        ob[1, at, :] = (full[1, at, :].astype(F32) + dx).astype(BF)
        return carry

    lax.fori_loop(0, 4, layer_back, 0)
    gin2 = back_stage2(1)

    sum_a = reduce_second(0, sum_a)
    arrived(res2)
    res1 = back_stage1(0)
    arrived(gin2)
    gin1 = back_stage1(1)
    sum_a = reduce_z(0, sum_a)
    sum_b = reduce_second(1, sum_b)
    arrived(res1)
    res_out[...] = fin[0]
    arrived(gin1)
    gin_out[...] = fin[1]
    sum_b = reduce_z(1, sum_b)
    arrived(sum_a)
    arrived(sum_b)
    total = zb[0, rows(z * 48, 48), :].astype(F32)
    for i in range(7):
        total = total + zr[i].astype(F32)
    sum_out[...] = total
    for copy in started:
        copy.wait_send()


N_COPY = 1 + 14 + 6 + 6 + 18 + 14 + 2 + 12 + 12 + 7 + 2 + 14 + 14


def body(tokens_in, mod_shift, mod_scale, branch_gate, inproj, outproj, norm_gain, grad_result):
    pad = jnp.zeros((D, W2 - 576), BF)
    weights = jnp.stack(
        [
            jnp.concatenate([inproj[:, 0], inproj[:, 2], pad], axis=1),
            jnp.concatenate([inproj[:, 1], outproj.T, pad], axis=1),
        ]
    )
    gains = jnp.pad(jnp.tile(norm_gain, (1, 4)), ((0, 0), (0, HW - 288)))
    swap, turn, first, second, upper, lower, heads = constants()
    vm = pl.BlockSpec(memory_space=pltpu.VMEM)
    anys = pl.BlockSpec(memory_space=pl.ANY)

    def vmem(shape, dtype=BF):
        return pltpu.VMEM(shape, dtype)

    result, grad_in, summed = pl.pallas_call(
        kernel,
        out_shape=(
            jax.ShapeDtypeStruct((128, D), BF),
            jax.ShapeDtypeStruct((128, D), BF),
            jax.ShapeDtypeStruct((48, W2), F32),
        ),
        in_specs=[vm] * 7 + [vm, anys] + [vm] * 5,
        out_specs=(vm, vm, vm),
        scratch_shapes=[
            vmem((D, D)),
            vmem((2, D, W2)),
            vmem((2, 128, D)),
            vmem((2, 128, D)),
            vmem((2, 256, D)),
            vmem((256, D)),
            vmem((D, 256)),
            vmem((D, 512)),
            vmem((256, D)),
            vmem((256, W2), F32),
            vmem((256, HW), F32),
            vmem((256, W2)),
            vmem((256, HW)),
            vmem((256, HW)),
            vmem((256, HW), F32),
            vmem((256, HW), F32),
            vmem((256, HW), F32),
            vmem((256, HW), F32),
            vmem((256, HW), F32),
            vmem((256, HW), F32),
            vmem((256, D), F32),
            vmem((256, D), F32),
            vmem((768, W2)),
            vmem((2, D, W2)),
            vmem((2, D, W2)),
            vmem((2, 2, 3, 288, W2)),
            vmem((2, 2, 3, 80, W2)),
            vmem((2, 2, 320, W2)),
            vmem((2, 192, W2)),
            vmem((7, 48, W2)),
            vmem((2, 128, D)),
            vmem((2, 128, D)),
            vmem((2, 128, D)),
            vmem((2, 128, D)),
            vmem((2, 128, D)),
            vmem((2, 128, D)),
            pltpu.SemaphoreType.DMA((1,)),
            pltpu.SemaphoreType.DMA((N_COPY,)),
            pltpu.SemaphoreType.DMA((N_COPY,)),
        ],
        compiler_params=pltpu.CompilerParams(
            collective_id=0, has_side_effects=True, vmem_limit_bytes=58 * 2**20
        ),
        name="sublayer",
    )(
        tokens_in, grad_result, mod_shift[None], mod_scale[None], branch_gate[None], gains,
        weights, swap, turn, first, second, upper, lower, heads,
    )
    grad_inproj = jnp.stack(
        [summed[0:18, 0:288], summed[18:36, 0:288], summed[0:18, 288:576]], axis=1
    )
    return result, grad_in, grad_inproj, summed[18:36, 288:576].T


def solution(mesh):
    placed = (
        P(("frame", "head"), None),
        P(),
        P(),
        P(),
        P(None, None, "head"),
        P("head", None),
        P(),
        P(("frame", "head"), None),
    )
    return jax.shard_map(
        body,
        mesh=mesh,
        in_specs=placed,
        out_specs=(
            P(("frame", "head"), None),
            P(("frame", "head"), None),
            P("frame", None, "head"),
            P("head", "frame"),
        ),
        check_vma=False,
    )
```

time: 1040 us -> 156 us (0.15); the launches traced: 1020 us -> 156 us
  waiting for transfers between devices: 850 us -> 0 us
  Pallas kernels: 0 us -> 139 us
  blocking collectives: 56.9 us -> 0 us
  local copies, waits for them, and re-layouts: 44.7 us -> 12.6 us
  matrix products: 20.9 us -> 0 us
  starting transfers between devices: 17.9 us -> 0 us
  other arithmetic: 19 us -> 3.32 us
  between operations: 14.7 us -> 0.71 us
    unnamed x6 -> x0, waiting for transfers between devices: 712 us -> none
    pallas_call x0 -> x1, Pallas kernels: none -> 139 us  [body(): pl.pallas_call(kernel, out_shape=(jax.ShapeDtypeStruct((128, D), BF), jax...]
    all_to_all x2 -> x0, blocking collectives: 56.9 us -> none  [the longest x1 36.7 us: body(): lax.all_to_all(grad_heads.reshape(FRAMES, 1, pixels_here, 3, width), 'fra...]
    all_gather x2 -> x0, waiting for transfers between devices: 56.7 us -> none  [the longest x1 31.8 us: body(): gathered = lax.all_gather(tokens_in, 'head', axis=0, tiled=True)]
    reduce_scatter x2 -> x0, waiting for transfers between devices: 48.8 us -> none  [the longest x1 43.7 us: body(): lax.psum_scatter(jnp.dot(block, outproj, preferred_element_type=jnp.float...]
    all_to_all x2 -> x0, waiting for transfers between devices: 32.8 us -> none  [the longest x1 26.6 us: body(): lax.all_to_all(split_rows, 'frame', split_axis=1, concat_axis=0, tiled=True)]
    dot_general x12 -> x0, matrix products: 20.9 us -> none  [the longest x1 3.61 us: body(): jnp.dot(grad_all.T, attended, preferred_element_type=jnp.float32)]
    all_to_all x2 -> x0, starting transfers between devices: 17.5 us -> none  [the longest x1 10.4 us: body(): lax.all_to_all(sent_grads, 'frame', split_axis=1, concat_axis=0, tiled=True)]
  transfers between devices with their start and end apart: 7 -> 0, of which waited for: 7 -> 0; matrix products, arithmetic and copies ran while one was open for 4% -> 0% of each run, Pallas kernels for 0% -> 0%
where the time goes in v1:
time: 156 us
  Pallas kernels  139 us (89%)
  local copies, waits for them, and re-layouts  12.6 us (8%)
  other arithmetic  3.32 us (2%)
    pallas_call x1, Pallas kernels, body(): pl.pallas_call(kernel, out_shape=(jax.ShapeDtypeStruct((128, D), BF), jax...  139 us
    unnamed x15, local copies, waits for them, and re-layouts  6.81 us
    another operation x2, other arithmetic, body(): jnp.stack([jnp.concatenate([inproj[:, 0], inproj[:, 2], pad], axis=1), jn...  3.31 us

profile of v1, /device:TPU:64, one launch (start us, length us, event | category | flops | bytes accessed | tf_op | source)
XLA Modules:
  0.0 155.8 jit_solution(4128703639779085011)
XLA Ops:
  0.6 1.6 %fusion = (bf16[1152,1,288]{0,2,1:T(8,128)(2,1)S(1)}, bf16[1152,1,288]{0,2,1:T(8,128)(2,1)S(1)}, bf16[1152,1,288]{0,2,1:T(8,128)(2,1)S(1)}) fusion(bf16[1152,3,288]{0,2,1:T(8,128)(2,1)} %param.19), kind=kLoop, calls=%fused_computation.8 | loop fusion | bytes 3981312 | tf_op jit(solution)/shard_map/slice | solution.py:463
  2.3 0.4 copy.24
  2.7 0.4 copy.25
  3.1 0.4 copy.26
  3.5 1.5 copy.22
  5.0 0.1 pad.15.clone
  5.1 1.4 maximum_bitcast_fusion
  6.5 0.0 copy-start.3
  6.5 0.0 copy-start
  6.5 0.0 copy-start.1
  6.5 0.0 copy-start.2
  6.5 1.9 %pad_maximum_fusion.wa = bf16[2,1152,640]{2,1,0:T(8,128)(2,1)} fusion(bf16[1,1152,640]{2,1,0:T(8,128)(2,1)S(1)} %get-tuple-element.22, bf16[1,1152,640]{2,1,0:T(8,128)(2,1)S(1)} %get-tuple-element.21), kind=kLoop, calls=%fused_computation | loop fusion | flops 1474560 | bytes 5898240 | tf_op jit(solution)/shard_map/stack | solution.py:461
  8.5 0.0 copy-done.3
  8.5 0.1 tile.10
  8.6 0.6 pad.4.gains
  9.1 0.0 copy-done
  9.1 0.6 broadcast_in_dim.12.shift
  9.7 0.0 copy-done.1
  9.7 0.6 broadcast_in_dim.13.scale
  10.3 0.0 copy-done.2
  10.3 0.6 broadcast_in_dim.14.gate
  10.9 139.2 %sublayer.1 = (bf16[128,1152]{1,0:T(8,128)(2,1)}, bf16[128,1152]{1,0:T(8,128)(2,1)}, f32[48,640]{1,0:T(8,128)}) custom-call(bf16[128,1152]{1,0:T(8,128)(2,1)} %tok.1, bf16[128,1152]{1,0:T(8,128)(2,1)} %grd.1, f32[1,1152]{1,0:T(1,128)} %broadcast_in_dim.12.shift, f32[1,1152]{1,0:T(1,128)} %broadcast_in_dim.13.scale, f32[1,1152]{1,0:T(1,128)} %broadcast_in_dim.14.gate, ...), custom_call_target="tpu_custom_call" | custom-call | tf_op jit(solution)/shard_map/sublayer/pallas_call | solution.py:475
  150.1 1.6 %slice_bitcast_fusion = (f32[288,18]{0,1:T(8,128)}, f32[18,1,288]{2,0,1:T(8,128)S(1)}, f32[18,1,288]{2,0,1:T(8,128)S(1)}, f32[18,1,288]{2,0,1:T(8,128)S(1)}) fusion(f32[48,640]{1,0:T(8,128)} %get-tuple-element.9), kind=kLoop, calls=%fused_computation.4 | loop fusion | bytes 165888 | tf_op jit(solution)/shard_map/transpose | solution.py:536
  151.7 0.7 copy.23
  152.4 1.7 %copy.29 = bf16[128,1152]{1,0:T(8,128)(2,1)} copy(bf16[128,1152]{1,0:T(8,128)(2,1)} %get-tuple-element.27) | data formatting | bytes 589824
  154.1 1.7 %copy.30 = bf16[128,1152]{1,0:T(8,128)(2,1)} copy(bf16[128,1152]{1,0:T(8,128)(2,1)} %get-tuple-element.28) | data formatting | bytes 589824
  (3 shorter events, 0.0 us)
Async XLA Ops:
  6.5 2.0 %copy-start.3 = (f32[2,72]{1,0:T(2,128)S(1)}, f32[2,72]{1,0:T(2,128)}, u32[]{:S(2)}) copy-start(f32[2,72]{1,0:T(2,128)} %param.21) | copy-start | bytes 1732
  6.5 2.6 %copy-start = (f32[1152]{0:T(1024)S(1)}, f32[1152]{0:T(1024)}, u32[]{:S(2)}) copy-start(f32[1152]{0:T(1024)} %param.16) | copy-start | bytes 13828
  6.5 3.2 %copy-start.1 = (f32[1152]{0:T(1024)S(1)}, f32[1152]{0:T(1024)}, u32[]{:S(2)}) copy-start(f32[1152]{0:T(1024)} %param.17) | copy-start | bytes 13828
  6.5 3.8 %copy-start.2 = (f32[1152]{0:T(1024)S(1)}, f32[1152]{0:T(1024)}, u32[]{:S(2)}) copy-start(f32[1152]{0:T(1024)} %param.18) | copy-start | bytes 13828

commit v2 on v1

v2 whole, which is shorter than its diff:
```python
import functools

import jax
import jax.numpy as jnp
import ml_dtypes
import numpy as np
from jax import lax
from jax.experimental import pallas as pl
from jax.experimental.pallas import tpu as pltpu
from jax.sharding import PartitionSpec as P

D = 1152
HD = 72
W2 = 640
W1 = D - W2
HC = 288
BF = jnp.bfloat16
F32 = jnp.float32
MESH = pl.DeviceIdType.MESH

def one_hot(rows, cols, source):
    made = np.zeros((rows, cols), np.float32)
    for row in range(rows):
        col = source(row)
        if col is not None:
            made[row, col] = 1.0
    return made.astype(ml_dtypes.bfloat16)


def constants():
    swap = one_hot(128, 128, lambda o: (o // 2 % 8) * 16 + (o // 16) * 2 + o % 2)
    turn = one_hot(
        D, D, lambda t: (t % 288 // 72) * 288 + (t % 72 // 18) * 72 + (t // 288) * 18 + t % 18
    )
    first = one_hot(
        320,
        288,
        lambda o: (o % 80 // 18) * 72 + (o // 80) * 18 + o % 80 % 18 if o % 80 < 72 else None,
    )
    second = one_hot(320, 288, lambda o: (o // 80) * 72 + o % 80 if o % 80 < 72 else None)
    upper = one_hot(192, 80, lambda o: (o // 48) * 18 + o % 48 if o % 48 < 18 else None)
    lower = one_hot(
        192, 80, lambda o: (o // 48) * 18 + o % 48 - 18 if 18 <= o % 48 < 36 else None
    )
    heads = np.zeros((HC, HC), np.float32)
    for h in range(4):
        heads[h * HD : (h + 1) * HD, h * HD : (h + 1) * HD] = 1.0
    return (swap, turn, first, second, upper, lower, heads.astype(ml_dtypes.bfloat16))


def mm(a, b):
    return jnp.dot(a, b, preferred_element_type=F32)


def mm_nt(a, b):
    return lax.dot_general(a, b, (((1,), (1,)), ((), ())), preferred_element_type=F32)


def mm_tn(a, b):
    return lax.dot_general(a, b, (((0,), (0,)), ((), ())), preferred_element_type=F32)


def head_sum(values, ones):
    high = values.astype(BF)
    low = (values - high.astype(F32)).astype(BF)
    return mm(high, ones) + mm(low, ones)


def kernel(
    tok, grd, shift_in, scale_in, gate_in, gain_in, w_in, w_out, swap, turn_hbm, first, second,
    upper, lower, heads,
    res_out, gin_out, inproj_out, outproj_out,
    wown, turn, wo, r1, per, full, mod, mod_t, both_t, gs, qf, kf, qn, kn, vn, ga, rq, rk,
    acc_o, acc_q, acc_k, acc_v, ao, gm, gx1, gx2, g1, g2, m1, s1, q1, m2, s2, zb, zr, cs, cr,
    ob, back, backp, fin,
    local_sem, ssem, rsem,
):
    f = lax.axis_index("frame")
    h = lax.axis_index("head")
    x, z, yh, yl = f // 16, (f // 4) % 4, (f // 2) % 2, f % 2
    zh, c = h // 2, h % 2
    y = yh * 2 + yl

    def dev(px=x, pz=z, py=y, ph=zh, pc=c):
        return ((px * 4 + pz) * 4 + py, ph * 2 + pc)

    def flip(dh, dl):
        return ((yh + dh) % 2) * 2 + (yl + dl) % 2

    stage1_to = [dev(pz=(z + dz) % 4, py=flip(dh, 0)) for dz in range(4) for dh in range(2)]
    stage1_at = [((z + dz) % 4) * 2 + (yh + dh) % 2 for dz in range(4) for dh in range(2)]
    stage1_from = [dev(pz=(z - dz) % 4, py=flip(dh, 0)) for dz in range(4) for dh in range(2)]
    stage2_to = [dev(px=(x + dx) % 4, py=flip(0, dl)) for dx in range(4) for dl in range(2)]
    stage2_at = [((x + dx) % 4) * 2 + (yl + dl) % 2 for dx in range(4) for dl in range(2)]
    stage2_from = [dev(px=(x - dx) % 4, py=flip(0, dl)) for dx in range(4) for dl in range(2)]
    core = dev(pc=1 - c)
    mirror = dev(pz=3 - z, ph=1 - zh)
    z_other = [dev(pz=(z + dz) % 4, ph=1 - zh) for dz in range(4)]
    z_same = [dev(pz=(z + dz) % 4) for dz in (1, 2, 3)]
    partners = stage1_to[1:] + stage2_to[1:] + [dev(py=flip(1, 1)), core] + z_other

    count = [0]
    started = []

    def send(src, dst, to):
        at = count[0]
        count[0] += 1
        copy = pltpu.make_async_remote_copy(
            src_ref=src, dst_ref=dst, send_sem=ssem.at[at], recv_sem=rsem.at[at],
            device_id=to, device_id_type=MESH,
        )
        copy.start()
        started.append(copy)
        return copy

    def rows(start, size):
        return pl.ds(pl.multiple_of(start, 16), size)

    def arrived(copies):
        for copy in copies:
            copy.wait_recv()

    load_in = pltpu.make_async_copy(w_in, wown.at[pl.ds(0, 864)], local_sem.at[0])
    load_out = pltpu.make_async_copy(w_out, wown.at[pl.ds(864, HC)], local_sem.at[1])
    load_turn = pltpu.make_async_copy(turn_hbm, turn, local_sem.at[2])
    load_in.start()
    load_out.start()
    load_turn.start()

    barrier = pltpu.get_barrier_semaphore()
    for to in partners:
        pl.semaphore_signal(barrier, inc=1, device_id=to, device_id_type=MESH)
    pl.semaphore_wait(barrier, len(partners))

    def stage1(src, which):
        out = []
        for slot in range(8):
            block = rows(stage1_at[slot] * 16, 16)
            if slot == 0:
                r1[which, 0:16, :] = src[block, :]
            else:
                out.append(
                    send(src.at[block], r1.at[which, pl.ds(slot * 16, 16)], stage1_to[slot])
                )
        return out

    def stage2(which):
        per[which] = mm(swap[...], r1[which]).astype(BF)
        out = []
        for slot in range(8):
            block = rows(stage2_at[slot] * 16, 16)
            if slot == 0:
                full[which, 0:16, :] = per[which, block, :]
            else:
                out.append(
                    send(
                        per.at[which, block],
                        full.at[which, pl.ds(slot * 16, 16)],
                        stage2_to[slot],
                    )
                )
        return out

    def to_core(which):
        return send(full.at[which, pl.ds(0, 128)], full.at[which, pl.ds(128, 128)], core)

    tok1 = stage1(tok, 0)

    def piece(px, py):
        return py % 2, (px * 2 + py // 2) * 144

    part, start = piece(x, y)
    load_in.wait()
    load_out.wait()
    w_z = send(
        wown.at[rows(start, 144), pl.ds(pl.multiple_of(part * 512, 128), W2)],
        wo.at[part, rows(start, 144)],
        mirror,
    )
    grd1 = stage1(grd, 1)

    def over_x(pc, st):
        ref = wo.at[pc, rows(st + 80, 64)]
        return [send(ref, ref, dev(px=(x + dx) % 4)) for dx in (1, 2, 3)]

    def over_y(pc, st):
        ref = wo.at[pc, rows(st, 80)]
        return [send(ref, ref, dev(py=flip(*d))) for d in ((0, 1), (1, 0), (1, 1))]

    arrived(tok1)
    tok2 = stage2(0)
    w_z.wait_recv()
    first_x = wo.at[part, rows(start, 80)]
    w_x1 = [send(first_x, first_x, dev(px=(x + dx) % 4)) for dx in (1, 2, 3)]
    first_y = wo.at[part, rows(start + 80, 64)]
    w_y1 = [send(first_y, first_y, dev(py=flip(*d))) for d in ((0, 1), (1, 0), (1, 1))]
    w_last = over_y(part, start) + over_x(part, start)
    arrived(grd1)
    grd2 = stage2(1)
    arrived(tok2)
    tok3 = to_core(0)
    load_turn.wait()
    tok3.wait_recv()

    shift = shift_in[...].reshape(1, D)
    scale = scale_in[...].reshape(1, D)
    gate = gate_in[...].reshape(1, D)

    def modulate(i, carry):
        at = pl.ds(pl.multiple_of(i * 32, 32), 32)
        field = full[0, at, :].astype(F32)
        mean = jnp.mean(field, axis=-1, keepdims=True)
        centred = field - mean
        spread = jnp.mean(centred * centred, axis=-1, keepdims=True)
        mod[at, :] = (centred * lax.rsqrt(spread + 1e-06) * (1.0 + scale) + shift).astype(BF)
        return carry

    lax.fori_loop(0, 8, modulate, 0)

    for copy, dx in zip(w_x1, (1, 2, 3)):
        copy.wait_recv()
        w_last += over_y(*piece((x - dx) % 4, y))
    for copy, d in zip(w_y1, ((0, 1), (1, 0), (1, 1))):
        copy.wait_recv()
        w_last += over_x(*piece(x, flip(*d)))

    lane = lax.broadcasted_iota(jnp.int32, (1, HC), 1)
    row_i = lax.broadcasted_iota(jnp.int32, (256, 256), 0)
    col_i = lax.broadcasted_iota(jnp.int32, (256, 256), 1)
    gain_q = jnp.concatenate([gain_in[0:1, :]] * 4, axis=1)
    gain_k = jnp.concatenate([gain_in[1:2, :]] * 4, axis=1)

    def own(j):
        at = pl.ds(j * HC, HC)
        return wown[at, 0:W2], wown[at, W2:D]

    def other(j):
        at = pl.ds(j * HC, HC)
        return wo[0, at, :], wo[1, at, W2 - W1 : W2]

    def project(act, w, j):
        low, high = w(j)
        return mm_nt(act[:, 0:W2], low) + mm_nt(act[:, W2:D], high)

    def forward(w):
        q = project(mod, w, 0)
        qf[...] = q
        r = lax.rsqrt(head_sum(q * q, heads[...]) * (1.0 / HD) + 1e-06)
        rq[...] = r
        qn[...] = (q * r * gain_q).astype(BF)
        k = project(mod, w, 1)
        kf[...] = k
        r = lax.rsqrt(head_sum(k * k, heads[...]) * (1.0 / HD) + 1e-06)
        rk[...] = r
        kn[...] = (k * r * gain_k).astype(BF)
        vn[...] = project(mod, w, 2).astype(BF)

    def cotangent(w):
        ga[...] = project(gs, w, 3).astype(BF)

    def attention():
        acc_o[...] = jnp.zeros_like(acc_o)
        acc_q[...] = jnp.zeros_like(acc_q)
        acc_k[...] = jnp.zeros_like(acc_k)
        acc_v[...] = jnp.zeros_like(acc_v)
        same = (row_i // 128 == col_i // 128) & (row_i % 2 == col_i % 2)
        root = 1.0 / np.sqrt(np.float32(HD))

        def head(i, carry):
            inside = (lane >= i * HD) & (lane < i * HD + HD)
            zero = jnp.zeros((), BF)
            qh = jnp.where(inside, qn[...], zero)
            kh = jnp.where(inside, kn[...], zero)
            vh = jnp.where(inside, vn[...], zero)
            gh = jnp.where(inside, ga[...], zero)
            s = jnp.where(same, mm_nt(qh, kh) * root, -1e30)
            e = jnp.exp(s - jnp.max(s, axis=-1, keepdims=True))
            p = e * (1.0 / jnp.sum(e, axis=-1, keepdims=True))
            pb = p.astype(BF)
            acc_o[...] += mm(pb, vh)
            acc_v[...] += mm_tn(pb, gh)
            dp = mm_nt(gh, vh)
            ds = (p * (dp - jnp.sum(p * dp, axis=-1, keepdims=True)) * root).astype(BF)
            acc_q[...] += mm(ds, kh)
            acc_k[...] += mm_tn(ds, qh)
            return carry

        lax.fori_loop(0, 4, head, 0)

    def unnorm(cot, raw, r, gain):
        n = raw * r
        dn = cot.astype(BF).astype(F32) * gain
        inner = head_sum(n * dn, heads[...]) * (1.0 / HD)
        return (r * (dn - n * inner)).astype(BF)

    def grads(g):
        gq = unnorm(acc_q[...], qf[...], rq[...], gain_q)
        gk = unnorm(acc_k[...], kf[...], rk[...], gain_k)
        gv = acc_v[...].astype(BF)
        att = acc_o[...].astype(BF)
        pad = jnp.zeros((256, W2 - 2 * HC), BF)
        gx1[...] = jnp.concatenate([gq, gv, pad], axis=1)
        gx2[0:256, :] = jnp.concatenate([gk, jnp.zeros((256, W2 - HC), BF)], axis=1)
        gx2[256:512, :] = jnp.concatenate([jnp.zeros((256, HC), BF), att, pad], axis=1)

        def block(i, carry):
            at = pl.ds(pl.multiple_of(i * 288, 288), 288)
            g1[g, at, :] = mm(mod_t[at, :], gx1[...]).astype(BF)
            g2[g, at, :] = mm(both_t[at, :], gx2[...]).astype(BF)
            return carry

        lax.fori_loop(0, 4, block, 0)
        return gq, gk, gv, att

    def shares(g, w, parts):
        gq, gk, gv, att = parts
        (q0, q1_), (k0, k1_), (v0, v1_), (o0, o1_) = w(0), w(1), w(2), w(3)
        pieces = (
            (ao, pl.ds(0, W2), mm(att, o0)),
            (ao, pl.ds(W2, W1), mm(att, o1_)),
            (gm, pl.ds(0, W2), mm(gq, q0) + mm(gk, k0) + mm(gv, v0)),
            (gm, pl.ds(W2, W1), mm(gq, q1_) + mm(gk, k1_) + mm(gv, v1_)),
        )
        for ref, at, value in pieces:
            if g == 0:
                ref[:, at] = value
            else:
                ref[:, at] += value

    axes = (
        (x, dev(px=(x + 1) % 4), dev(px=(x - 1) % 4)),
        (y, dev(py=(y + 1) % 4), dev(py=(y - 1) % 4)),
    )

    def ring_start(ref, land, axis, size, cut):
        me, right, left = axes[axis]
        a = lambda k: ref.at[rows((me + k) % 4 * size, cut)]
        b = lambda k: ref.at[rows((me + k) % 4 * size + cut, size - cut)]
        top, low = pl.ds(0, cut), pl.ds(0, size - cut)
        return [
            send(a(2), land.at[0, top], right),
            send(b(2), land.at[1, low], left),
            send(b(1), land.at[2, low], right),
            send(a(3), land.at[3, top], left),
        ]

    def ring_middle(ref, land, merged, axis, size, cut, copies):
        me, right, left = axes[axis]
        top, low = pl.ds(0, cut), pl.ds(0, size - cut)
        copies[0].wait_recv()
        merged[0, top, :] = (
            ref[rows((me + 1) % 4 * size, cut), :].astype(F32) + land[0, top, :].astype(F32)
        ).astype(BF)
        out = [send(merged.at[0, top], land.at[4, top], right)]
        copies[1].wait_recv()
        merged[1, low, :] = (
            ref[rows((me + 3) % 4 * size + cut, size - cut), :].astype(F32)
            + land[1, low, :].astype(F32)
        ).astype(BF)
        out.append(send(merged.at[1, low], land.at[5, low], left))
        return copies + out

    def ring_end(ref, land, axis, size, cut, copies):
        me = axes[axis][0]
        top, low = pl.ds(0, cut), pl.ds(0, size - cut)
        arrived(copies[2:])
        a = ref[rows(me * size, cut), :].astype(F32)
        a = a + land[3, top, :].astype(F32) + land[4, top, :].astype(F32)
        b = ref[rows(me * size + cut, size - cut), :].astype(F32)
        b = b + land[2, low, :].astype(F32) + land[5, low, :].astype(F32)
        return a.astype(BF), b.astype(BF)

    def sum_start(g):
        return [
            ring_start(ref.at[g], s1.at[g, half], half, 288, 144)
            for half, ref in enumerate((g1, g2))
        ]

    def sum_middle(g, copies):
        return [
            ring_middle(ref.at[g], s1.at[g, half], m1.at[g, half], half, 288, 144, copies[half])
            for half, ref in enumerate((g1, g2))
        ]

    def second_start(g, copies):
        out = []
        for half, (ref, spread) in enumerate(((g1, first), (g2, second))):
            a, b = ring_end(ref.at[g], s1.at[g, half], half, 288, 144, copies[half])
            q1[g, half] = (mm(spread[:, 0:144], a) + mm(spread[:, 144:288], b)).astype(BF)
            out.append(ring_start(q1.at[g, half], s2.at[g, half], 1 - half, 80, 48))
        return out

    def second_middle(g, copies):
        return [
            ring_middle(
                q1.at[g, half], s2.at[g, half], m2.at[g, half], 1 - half, 80, 48, copies[half]
            )
            for half in range(2)
        ]

    def z_start(g, copies):
        total = 0.0
        for half, spread in enumerate((upper, lower)):
            a, b = ring_end(q1.at[g, half], s2.at[g, half], 1 - half, 80, 48, copies[half])
            total = total + mm(spread[:, 0:48], a) + mm(spread[:, 48:80], b)
        zb[g] = total.astype(BF)
        if g == 0:
            return [
                send(zb.at[0, rows((z + dz) % 4 * 48, 48)], zr.at[dz - 1], z_same[dz - 1])
                for dz in (1, 2, 3)
            ]
        return [
            send(zb.at[1, rows((z + dz) % 4 * 48, 48)], zr.at[3 + dz], z_other[dz])
            for dz in range(4)
        ]

    mod_t[...] = mod[...].T
    both_t[:, 0:256] = mm(turn[...], mod_t[...]).astype(BF)
    forward(own)
    arrived(grd2)
    to_core(1).wait_recv()
    gs[...] = (full[1].astype(F32) * gate).astype(BF)
    both_t[:, 256:512] = mm(turn[...], gs[...].T).astype(BF)
    cotangent(own)
    attention()
    made = grads(0)
    sum_a = sum_start(0)
    shares(0, own, made)
    arrived(w_last)
    forward(other)
    cotangent(other)
    sum_a = sum_middle(0, sum_a)
    attention()
    made = grads(1)
    sum_b = sum_start(1)
    sum_a = second_start(0, sum_a)
    shares(1, other, made)

    cs[0] = ao[128:256, :].astype(BF)
    cs[1] = gm[128:256, :].astype(BF)
    swapped = [send(cs.at[i], cr.at[i], core) for i in range(2)]
    sum_b = sum_middle(1, sum_b)
    sum_a = second_middle(0, sum_a)

    def back_stage2(which):
        block = rows((x * 2 + yl) * 16, 16)
        back[which, block, :] = ob[which, 0:16, :]
        return [
            send(ob.at[which, pl.ds(slot * 16, 16)], back.at[which, block], stage2_from[slot])
            for slot in range(1, 8)
        ]

    def back_stage1(which):
        backp[which] = mm(swap[...], back[which]).astype(BF)
        block = rows((z * 2 + yh) * 16, 16)
        fin[which, block, :] = backp[which, 0:16, :]
        return [
            send(backp.at[which, pl.ds(slot * 16, 16)], fin.at[which, block], stage1_from[slot])
            for slot in range(1, 8)
        ]

    swapped[0].wait_recv()
    ob[0] = (
        full[0, 0:128, :].astype(F32) + gate * (ao[0:128, :] + cr[0].astype(F32))
    ).astype(BF)
    res2 = back_stage2(0)
    swapped[1].wait_recv()

    def layer_back(i, carry):
        at = pl.ds(pl.multiple_of(i * 32, 32), 32)
        field = full[0, at, :].astype(F32)
        mean = jnp.mean(field, axis=-1, keepdims=True)
        centred = field - mean
        spread = jnp.mean(centred * centred, axis=-1, keepdims=True)
        r = lax.rsqrt(spread + 1e-06)
        hat = centred * r
        d = (gm[at, :] + cr[1, at, :].astype(F32)) * (1.0 + scale)
        dx = r * (
            d
            - jnp.mean(d, axis=-1, keepdims=True)
            - hat * jnp.mean(d * hat, axis=-1, keepdims=True)
        )
        ob[1, at, :] = (full[1, at, :].astype(F32) + dx).astype(BF)
        return carry

    lax.fori_loop(0, 4, layer_back, 0)
    gin2 = back_stage2(1)
    sum_a = z_start(0, sum_a)
    arrived(res2)
    res1 = back_stage1(0)
    sum_b = second_start(1, sum_b)
    arrived(gin2)
    gin1 = back_stage1(1)
    sum_b = second_middle(1, sum_b)
    sum_b = z_start(1, sum_b)
    arrived(res1)
    res_out[...] = fin[0]
    arrived(gin1)
    gin_out[...] = fin[1]
    arrived(sum_a)
    arrived(sum_b)
    total = zb[0, rows(z * 48, 48), :].astype(F32)
    for i in range(7):
        total = total + zr[i].astype(F32)
    inproj_out[:, 0, :] = total[0:18, 0:HC]
    inproj_out[:, 1, :] = total[18:36, 0:HC]
    inproj_out[:, 2, :] = total[0:18, HC : 2 * HC]
    outproj_out[...] = total[18:36, HC : 2 * HC]
    for copy in started:
        copy.wait_send()


N_COPY = 160


def body(tokens_in, mod_shift, mod_scale, branch_gate, inproj, outproj, norm_gain, grad_result):
    swap, turn, first, second, upper, lower, heads = constants()
    vm = pl.BlockSpec(memory_space=pltpu.VMEM)
    anys = pl.BlockSpec(memory_space=pl.ANY)

    def vmem(shape, dtype=BF):
        return pltpu.VMEM(shape, dtype)

    result, grad_in, grad_inproj, grad_outproj = pl.pallas_call(
        kernel,
        out_shape=(
            jax.ShapeDtypeStruct((128, D), BF),
            jax.ShapeDtypeStruct((128, D), BF),
            jax.ShapeDtypeStruct((18, 3, HC), F32),
            jax.ShapeDtypeStruct((18, HC), F32),
        ),
        in_specs=[vm] * 6 + [anys] * 2 + [vm, anys] + [vm] * 5,
        out_specs=(vm, vm, vm, vm),
        scratch_shapes=[
            vmem((D, D)),
            vmem((D, D)),
            vmem((2, D, W2)),
            vmem((2, 128, D)),
            vmem((2, 128, D)),
            vmem((2, 256, D)),
            vmem((256, D)),
            vmem((D, 256)),
            vmem((D, 512)),
            vmem((256, D)),
            vmem((256, HC), F32),
            vmem((256, HC), F32),
            vmem((256, HC)),
            vmem((256, HC)),
            vmem((256, HC)),
            vmem((256, HC)),
            vmem((256, HC), F32),
            vmem((256, HC), F32),
            vmem((256, HC), F32),
            vmem((256, HC), F32),
            vmem((256, HC), F32),
            vmem((256, HC), F32),
            vmem((256, D), F32),
            vmem((256, D), F32),
            vmem((256, W2)),
            vmem((512, W2)),
            vmem((2, D, W2)),
            vmem((2, D, W2)),
            vmem((2, 2, 2, 144, W2)),
            vmem((2, 2, 6, 144, W2)),
            vmem((2, 2, 320, W2)),
            vmem((2, 2, 2, 48, W2)),
            vmem((2, 2, 6, 48, W2)),
            vmem((2, 192, W2)),
            vmem((7, 48, W2)),
            vmem((2, 128, D)),
            vmem((2, 128, D)),
            vmem((2, 128, D)),
            vmem((2, 128, D)),
            vmem((2, 128, D)),
            vmem((2, 128, D)),
            pltpu.SemaphoreType.DMA((3,)),
            pltpu.SemaphoreType.DMA((N_COPY,)),
            pltpu.SemaphoreType.DMA((N_COPY,)),
        ],
        compiler_params=pltpu.CompilerParams(
            collective_id=0, has_side_effects=True, vmem_limit_bytes=58 * 2**20
        ),
        name="sublayer",
    )(
        tokens_in, grad_result, mod_shift, mod_scale, branch_gate, norm_gain,
        jnp.transpose(inproj, (1, 2, 0)).reshape(3 * HC, D), outproj,
        swap, turn, first, second, upper, lower, heads,
    )
    return result, grad_in, grad_inproj, grad_outproj.T


def solution(mesh):
    placed = (
        P(("frame", "head"), None),
        P(),
        P(),
        P(),
        P(None, None, "head"),
        P("head", None),
        P(),
        P(("frame", "head"), None),
    )
    return jax.shard_map(
        body,
        mesh=mesh,
        in_specs=placed,
        out_specs=(
            P(("frame", "head"), None),
            P(("frame", "head"), None),
            P("frame", None, "head"),
            P("head", "frame"),
        ),
        check_vma=False,
    )
```

time: 156 us -> 121 us (0.78)
  the two profiles are of different devices: /device:TPU:64 before, /device:TPU:1 now
where the time goes in v2:
time: 121 us; the launch traced here: 120 us
  Pallas kernels  113 us (93%)
  local copies, waits for them, and re-layouts  6.34 us (5%)
    pallas_call x1, Pallas kernels, body(): pl.pallas_call(kernel, out_shape=(jax.ShapeDtypeStruct((128, D), BF), jax...  113 us
    unnamed x4, local copies, waits for them, and re-layouts  6.34 us

profile of v2, /device:TPU:1, one launch (start us, length us, event | category | flops | bytes accessed | tf_op | source)
XLA Modules:
  0.0 120.3 jit_solution(17336123592241774641)
XLA Ops:
  0.6 113.4 %sublayer.1 = (bf16[128,1152]{1,0:T(8,128)(2,1)}, bf16[128,1152]{1,0:T(8,128)(2,1)}, f32[18,3,288]{2,1,0:T(4,128)}, f32[18,288]{1,0:T(8,128)}) custom-call(bf16[128,1152]{1,0:T(8,128)(2,1)} %tok.1, bf16[128,1152]{1,0:T(8,128)(2,1)} %grd.1, f32[1152]{0:T(1024)} %shift_in.1, f32[1152]{0:T(1024)} %scale_in.1, f32[1152]{0:T(1024)} %gate_in.1, f32[2,72]{1,0:T(2,128)} %gain_in.1, ...), custom_call_target="tpu_custom_call" | custom-call | tf_op jit(solution)/shard_map/sublayer/pallas_call | solution.py:524
  114.0 1.7 %copy.23 = bf16[128,1152]{1,0:T(8,128)(2,1)} copy(bf16[128,1152]{1,0:T(8,128)(2,1)} %get-tuple-element.16) | data formatting | bytes 589824
  115.7 1.7 %copy.24 = bf16[128,1152]{1,0:T(8,128)(2,1)} copy(bf16[128,1152]{1,0:T(8,128)(2,1)} %get-tuple-element.17) | data formatting | bytes 589824
  117.4 1.6 %copy.25 = f32[18,3,288]{2,1,0:T(4,128)} copy(f32[18,3,288]{2,1,0:T(4,128)} %get-tuple-element.18) | data formatting | bytes 124416
  119.0 1.4 %copy.26 = f32[288,18]{0,1:T(8,128)} copy(f32[288,18]{0,1:T(8,128)} %bitcast.5) | data formatting | bytes 41472

commit v3 on v2

--- a/solution.py
+++ b/solution.py
@@ -67,11 +67,11 @@
 
 
 def kernel(
-    tok, grd, shift_in, scale_in, gate_in, gain_in, w_in, w_out, swap, turn_hbm, first, second,
-    upper, lower, heads,
+    tok, grd, shift_in, scale_in, gate_in, gain_in, swap, heads, w_in, w_out, turn_hbm,
+    first_hbm, second_hbm, upper_hbm, lower_hbm,
     res_out, gin_out, inproj_out, outproj_out,
-    wown, turn, wo, r1, per, full, mod, mod_t, both_t, gs, qf, kf, qn, kn, vn, ga, rq, rk,
-    acc_o, acc_q, acc_k, acc_v, ao, gm, gx1, gx2, g1, g2, m1, s1, q1, m2, s2, zb, zr, cs, cr,
+    wown, turn, first, second, upper, lower, wo, ta1, ta2, ga1, ga2, ga3, ga4, full, mod, mod_t, both_t, gs, qf, kf, qn, kn, vn, ga, rq, rk,
+    acc_o, acc_q, acc_k, acc_v, ao, gm, gx1, gx2, g1, g2, m1, s1, q1, s2, zb, zr, cs, cr,
     ob, back, backp, fin,
     local_sem, ssem, rsem,
 ):
@@ -120,88 +120,85 @@
         for copy in copies:
             copy.wait_recv()
 
-    load_in = pltpu.make_async_copy(w_in, wown.at[pl.ds(0, 864)], local_sem.at[0])
-    load_out = pltpu.make_async_copy(w_out, wown.at[pl.ds(864, HC)], local_sem.at[1])
-    load_turn = pltpu.make_async_copy(turn_hbm, turn, local_sem.at[2])
-    load_in.start()
-    load_out.start()
-    load_turn.start()
+    loads = [
+        pltpu.make_async_copy(src, dst, local_sem.at[i])
+        for i, (src, dst) in enumerate(
+            (
+                (w_in, wown.at[pl.ds(0, 864)]),
+                (w_out, wown.at[pl.ds(864, HC)]),
+                (turn_hbm, turn),
+                (first_hbm, first),
+                (second_hbm, second),
+                (upper_hbm, upper),
+                (lower_hbm, lower),
+            )
+        )
+    ]
+    for load in loads:
+        load.start()
 
     barrier = pltpu.get_barrier_semaphore()
     for to in partners:
         pl.semaphore_signal(barrier, inc=1, device_id=to, device_id_type=MESH)
+    ga1[...] = mm(swap[...], grd[...]).astype(BF)
+    loads[0].wait()
+    loads[1].wait()
     pl.semaphore_wait(barrier, len(partners))
 
-    def stage1(src, which):
+    def spread(src, dst, places, targets):
         out = []
         for slot in range(8):
-            block = rows(stage1_at[slot] * 16, 16)
+            block = rows(places[slot] * 16, 16)
             if slot == 0:
-                r1[which, 0:16, :] = src[block, :]
+                dst[0:16, :] = src[block, :]
             else:
-                out.append(
-                    send(src.at[block], r1.at[which, pl.ds(slot * 16, 16)], stage1_to[slot])
-                )
-        return out
-
-    def stage2(which):
-        per[which] = mm(swap[...], r1[which]).astype(BF)
-        out = []
-        for slot in range(8):
-            block = rows(stage2_at[slot] * 16, 16)
-            if slot == 0:
-                full[which, 0:16, :] = per[which, block, :]
-            else:
-                out.append(
-                    send(
-                        per.at[which, block],
-                        full.at[which, pl.ds(slot * 16, 16)],
-                        stage2_to[slot],
-                    )
-                )
+                out.append(send(src.at[block], dst.at[pl.ds(slot * 16, 16)], targets[slot]))
         return out
 
     def to_core(which):
         return send(full.at[which, pl.ds(0, 128)], full.at[which, pl.ds(128, 128)], core)
 
-    tok1 = stage1(tok, 0)
-
     def piece(px, py):
         return py % 2, (px * 2 + py // 2) * 144
 
     part, start = piece(x, y)
-    load_in.wait()
-    load_out.wait()
-    w_z = send(
-        wown.at[rows(start, 144), pl.ds(pl.multiple_of(part * 512, 128), W2)],
-        wo.at[part, rows(start, 144)],
-        mirror,
-    )
-    grd1 = stage1(grd, 1)
-
-    def over_x(pc, st):
-        ref = wo.at[pc, rows(st + 80, 64)]
+    lanes = pl.ds(pl.multiple_of(part * 512, 128), W2)
+    w_z = [
+        send(wown.at[rows(start + at, size), lanes], wo.at[part, rows(start + at, size)], mirror)
+        for at, size in ((0, 80), (80, 64))
+    ]
+    tok1 = spread(tok, ta1, stage1_at, stage1_to)
+    grd1 = spread(ga1, ga2, stage2_at, stage2_to)
+
+    flips = ((0, 1), (1, 0), (1, 1))
+
+    def over_x(pc, at, size):
+        ref = wo.at[pc, rows(at, size)]
         return [send(ref, ref, dev(px=(x + dx) % 4)) for dx in (1, 2, 3)]
 
-    def over_y(pc, st):
-        ref = wo.at[pc, rows(st, 80)]
-        return [send(ref, ref, dev(py=flip(*d))) for d in ((0, 1), (1, 0), (1, 1))]
-
+    def over_y(pc, at, size):
+        ref = wo.at[pc, rows(at, size)]
+        return [send(ref, ref, dev(py=flip(*d))) for d in flips]
+
+    arrived(grd1)
+    ga3[...] = mm(swap[...], ga2[...]).astype(BF)
+    grd2 = spread(ga3, ga4, stage1_at, stage1_to)
+    w_z[0].wait_recv()
+    w_x1 = over_x(part, start, 80)
+    w_z[1].wait_recv()
+    w_y1 = over_y(part, start + 80, 64)
     arrived(tok1)
-    tok2 = stage2(0)
-    w_z.wait_recv()
-    first_x = wo.at[part, rows(start, 80)]
-    w_x1 = [send(first_x, first_x, dev(px=(x + dx) % 4)) for dx in (1, 2, 3)]
-    first_y = wo.at[part, rows(start + 80, 64)]
-    w_y1 = [send(first_y, first_y, dev(py=flip(*d))) for d in ((0, 1), (1, 0), (1, 1))]
-    w_last = over_y(part, start) + over_x(part, start)
-    arrived(grd1)
-    grd2 = stage2(1)
-    arrived(tok2)
-    tok3 = to_core(0)
-    load_turn.wait()
-    tok3.wait_recv()
-
+    ta2[...] = mm(swap[...], ta1[...]).astype(BF)
+    tok2 = spread(ta2, full.at[0], stage2_at, stage2_to)
+    w_last = over_y(part, start, 80) + over_x(part, start + 80, 64)
+    for copy, dx in zip(w_x1, (1, 2, 3)):
+        copy.wait_recv()
+        pc, at = piece((x - dx) % 4, y)
+        w_last += over_y(pc, at, 80)
+    for copy, d in zip(w_y1, flips):
+        copy.wait_recv()
+        pc, at = piece(x, flip(*d))
+        w_last += over_x(pc, at + 80, 64)
     shift = shift_in[...].reshape(1, D)
     scale = scale_in[...].reshape(1, D)
     gate = gate_in[...].reshape(1, D)
@@ -215,14 +212,16 @@
         mod[at, :] = (centred * lax.rsqrt(spread + 1e-06) * (1.0 + scale) + shift).astype(BF)
         return carry
 
-    lax.fori_loop(0, 8, modulate, 0)
-
-    for copy, dx in zip(w_x1, (1, 2, 3)):
-        copy.wait_recv()
-        w_last += over_y(*piece((x - dx) % 4, y))
-    for copy, d in zip(w_y1, ((0, 1), (1, 0), (1, 1))):
-        copy.wait_recv()
-        w_last += over_x(*piece(x, flip(*d)))
+    arrived(tok2)
+    tok3 = to_core(0)
+    arrived(grd2)
+    full[1, 0:128, :] = mm(swap[...], ga4[...]).astype(BF)
+    grd3 = to_core(1)
+    lax.fori_loop(0, 4, modulate, 0)
+    tok3.wait_recv()
+    lax.fori_loop(4, 8, modulate, 0)
+    for load in loads[2:]:
+        load.wait()
 
     lane = lax.broadcasted_iota(jnp.int32, (1, HC), 1)
     row_i = lax.broadcasted_iota(jnp.int32, (256, 256), 0)
@@ -285,13 +284,84 @@
             acc_k[...] += mm_tn(ds, qh)
             return carry
 
-        lax.fori_loop(0, 4, head, 0)
+        lax.fori_loop(0, 4, head, 0, unroll=2)
 
     def unnorm(cot, raw, r, gain):
         n = raw * r
         dn = cot.astype(BF).astype(F32) * gain
         inner = head_sum(n * dn, heads[...]) * (1.0 / HD)
         return (r * (dn - n * inner)).astype(BF)
+
+    axes = (
+        (x, dev(px=(x + 1) % 4), dev(px=(x - 1) % 4)),
+        (y, dev(py=(y + 1) % 4), dev(py=(y - 1) % 4)),
+    )
+
+    def ring_send(ref, land, axis, k, copies):
+        me, right, left = axes[axis]
+        start = (me + k) % 4 * 288
+        top, low = ref.at[rows(start, 144)], ref.at[rows(start + 144, 144)]
+        if k == 2:
+            copies[0] = send(top, land.at[0], right)
+            copies[1] = send(low, land.at[1], left)
+        elif k == 1:
+            copies[2] = send(low, land.at[2], right)
+        elif k == 3:
+            copies[3] = send(top, land.at[3], left)
+
+    def ring_middle(ref, land, merged, axis, copies):
+        me, right, left = axes[axis]
+        for i, (at, to) in enumerate((((me + 1) % 4 * 288, right), ((me + 3) % 4 * 288 + 144, left))):
+            copies[i].wait_recv()
+            merged[i] = (ref[rows(at, 144), :].astype(F32) + land[i].astype(F32)).astype(BF)
+            copies.append(send(merged.at[i], land.at[4 + i], to))
+
+    def ring_end(ref, land, axis, copies):
+        me = axes[axis][0]
+        arrived(copies[2:])
+        a = ref[rows(me * 288, 144), :].astype(F32)
+        a = a + land[3].astype(F32) + land[4].astype(F32)
+        b = ref[rows(me * 288 + 144, 144), :].astype(F32)
+        b = b + land[2].astype(F32) + land[5].astype(F32)
+        return a.astype(BF), b.astype(BF)
+
+    def sum_middle(g, copies):
+        for half, ref in enumerate((g1, g2)):
+            ring_middle(ref.at[g], s1.at[g, half], m1.at[g, half], half, copies[half])
+
+    def second_start(g, copies):
+        out = []
+        for half, (ref, spread) in enumerate(((g1, first), (g2, second))):
+            a, b = ring_end(ref.at[g], s1.at[g, half], half, copies[half])
+            q1[g, half] = (mm(spread[:, 0:144], a) + mm(spread[:, 144:288], b)).astype(BF)
+            if half == 0:
+                to = [(flip(*d), dev(py=flip(*d))) for d in flips]
+            else:
+                to = [((x + dx) % 4, dev(px=(x + dx) % 4)) for dx in (1, 2, 3)]
+            out += [
+                send(q1.at[g, half, rows(at * 80, 80)], s2.at[g, half, i], target)
+                for i, (at, target) in enumerate(to)
+            ]
+        return out
+
+    def z_start(g, copies):
+        arrived(copies)
+        total = 0.0
+        for half, (spread, me) in enumerate(((upper, y), (lower, x))):
+            part = q1[g, half, rows(me * 80, 80), :].astype(F32)
+            for i in range(3):
+                part = part + s2[g, half, i].astype(F32)
+            total = total + mm(spread[...], part.astype(BF))
+        zb[g] = total.astype(BF)
+        if g == 0:
+            return [
+                send(zb.at[0, rows((z + dz) % 4 * 48, 48)], zr.at[dz - 1], z_same[dz - 1])
+                for dz in (1, 2, 3)
+            ]
+        return [
+            send(zb.at[1, rows((z + dz) % 4 * 48, 48)], zr.at[3 + dz], z_other[dz])
+            for dz in range(4)
+        ]
 
     def grads(g):
         gq = unnorm(acc_q[...], qf[...], rq[...], gain_q)
@@ -303,14 +373,14 @@
         gx2[0:256, :] = jnp.concatenate([gk, jnp.zeros((256, W2 - HC), BF)], axis=1)
         gx2[256:512, :] = jnp.concatenate([jnp.zeros((256, HC), BF), att, pad], axis=1)
 
-        def block(i, carry):
-            at = pl.ds(pl.multiple_of(i * 288, 288), 288)
-            g1[g, at, :] = mm(mod_t[at, :], gx1[...]).astype(BF)
-            g2[g, at, :] = mm(both_t[at, :], gx2[...]).astype(BF)
-            return carry
-
-        lax.fori_loop(0, 4, block, 0)
-        return gq, gk, gv, att
+        copies = [[None] * 4, [None] * 4]
+        for k in (2, 1, 3, 0):
+            for half, (ref, left, right) in enumerate(((g1, mod_t, gx1), (g2, both_t, gx2))):
+                at = rows((axes[half][0] + k) % 4 * 288, 288)
+                ref[g, at, :] = mm(left[at, :], right[...]).astype(BF)
+                ring_send(ref.at[g], s1.at[g, half], half, k, copies[half])
+        return copies, (gq, gk, gv, att)
+
 
     def shares(g, w, parts):
         gq, gk, gv, att = parts
@@ -327,135 +397,44 @@
             else:
                 ref[:, at] += value
 
-    axes = (
-        (x, dev(px=(x + 1) % 4), dev(px=(x - 1) % 4)),
-        (y, dev(py=(y + 1) % 4), dev(py=(y - 1) % 4)),
-    )
-
-    def ring_start(ref, land, axis, size, cut):
-        me, right, left = axes[axis]
-        a = lambda k: ref.at[rows((me + k) % 4 * size, cut)]
-        b = lambda k: ref.at[rows((me + k) % 4 * size + cut, size - cut)]
-        top, low = pl.ds(0, cut), pl.ds(0, size - cut)
-        return [
-            send(a(2), land.at[0, top], right),
-            send(b(2), land.at[1, low], left),
-            send(b(1), land.at[2, low], right),
-            send(a(3), land.at[3, top], left),
-        ]
-
-    def ring_middle(ref, land, merged, axis, size, cut, copies):
-        me, right, left = axes[axis]
-        top, low = pl.ds(0, cut), pl.ds(0, size - cut)
-        copies[0].wait_recv()
-        merged[0, top, :] = (
-            ref[rows((me + 1) % 4 * size, cut), :].astype(F32) + land[0, top, :].astype(F32)
-        ).astype(BF)
-        out = [send(merged.at[0, top], land.at[4, top], right)]
-        copies[1].wait_recv()
-        merged[1, low, :] = (
-            ref[rows((me + 3) % 4 * size + cut, size - cut), :].astype(F32)
-            + land[1, low, :].astype(F32)
-        ).astype(BF)
-        out.append(send(merged.at[1, low], land.at[5, low], left))
-        return copies + out
-
-    def ring_end(ref, land, axis, size, cut, copies):
-        me = axes[axis][0]
-        top, low = pl.ds(0, cut), pl.ds(0, size - cut)
-        arrived(copies[2:])
-        a = ref[rows(me * size, cut), :].astype(F32)
-        a = a + land[3, top, :].astype(F32) + land[4, top, :].astype(F32)
-        b = ref[rows(me * size + cut, size - cut), :].astype(F32)
-        b = b + land[2, low, :].astype(F32) + land[5, low, :].astype(F32)
-        return a.astype(BF), b.astype(BF)
-
-    def sum_start(g):
-        return [
-            ring_start(ref.at[g], s1.at[g, half], half, 288, 144)
-            for half, ref in enumerate((g1, g2))
-        ]
-
-    def sum_middle(g, copies):
-        return [
-            ring_middle(ref.at[g], s1.at[g, half], m1.at[g, half], half, 288, 144, copies[half])
-            for half, ref in enumerate((g1, g2))
-        ]
-
-    def second_start(g, copies):
-        out = []
-        for half, (ref, spread) in enumerate(((g1, first), (g2, second))):
-            a, b = ring_end(ref.at[g], s1.at[g, half], half, 288, 144, copies[half])
-            q1[g, half] = (mm(spread[:, 0:144], a) + mm(spread[:, 144:288], b)).astype(BF)
-            out.append(ring_start(q1.at[g, half], s2.at[g, half], 1 - half, 80, 48))
-        return out
-
-    def second_middle(g, copies):
-        return [
-            ring_middle(
-                q1.at[g, half], s2.at[g, half], m2.at[g, half], 1 - half, 80, 48, copies[half]
-            )
-            for half in range(2)
-        ]
-
-    def z_start(g, copies):
-        total = 0.0
-        for half, spread in enumerate((upper, lower)):
-            a, b = ring_end(q1.at[g, half], s2.at[g, half], 1 - half, 80, 48, copies[half])
-            total = total + mm(spread[:, 0:48], a) + mm(spread[:, 48:80], b)
-        zb[g] = total.astype(BF)
-        if g == 0:
-            return [
-                send(zb.at[0, rows((z + dz) % 4 * 48, 48)], zr.at[dz - 1], z_same[dz - 1])
-                for dz in (1, 2, 3)
-            ]
-        return [
-            send(zb.at[1, rows((z + dz) % 4 * 48, 48)], zr.at[3 + dz], z_other[dz])
-            for dz in range(4)
-        ]
-
     mod_t[...] = mod[...].T
     both_t[:, 0:256] = mm(turn[...], mod_t[...]).astype(BF)
     forward(own)
-    arrived(grd2)
-    to_core(1).wait_recv()
+    grd3.wait_recv()
     gs[...] = (full[1].astype(F32) * gate).astype(BF)
     both_t[:, 256:512] = mm(turn[...], gs[...].T).astype(BF)
     cotangent(own)
     attention()
-    made = grads(0)
-    sum_a = sum_start(0)
+    sum_a, made = grads(0)
     shares(0, own, made)
     arrived(w_last)
     forward(other)
     cotangent(other)
-    sum_a = sum_middle(0, sum_a)
+    sum_middle(0, sum_a)
     attention()
-    made = grads(1)
-    sum_b = sum_start(1)
-    sum_a = second_start(0, sum_a)
+    sum_b, made = grads(1)
     shares(1, other, made)
 
     cs[0] = ao[128:256, :].astype(BF)
     cs[1] = gm[128:256, :].astype(BF)
     swapped = [send(cs.at[i], cr.at[i], core) for i in range(2)]
-    sum_b = sum_middle(1, sum_b)
-    sum_a = second_middle(0, sum_a)
-
-    def back_stage2(which):
-        block = rows((x * 2 + yl) * 16, 16)
+    sum_a = second_start(0, sum_a)
+
+    def back_first(which):
+        ob[which] = mm(swap[...], ob[which]).astype(BF)
+        block = rows((z * 2 + yh) * 16, 16)
         back[which, block, :] = ob[which, 0:16, :]
         return [
-            send(ob.at[which, pl.ds(slot * 16, 16)], back.at[which, block], stage2_from[slot])
+            send(ob.at[which, pl.ds(slot * 16, 16)], back.at[which, block], stage1_from[slot])
             for slot in range(1, 8)
         ]
 
-    def back_stage1(which):
+    def back_last(which):
         backp[which] = mm(swap[...], back[which]).astype(BF)
-        block = rows((z * 2 + yh) * 16, 16)
+        block = rows((x * 2 + yl) * 16, 16)
         fin[which, block, :] = backp[which, 0:16, :]
         return [
-            send(backp.at[which, pl.ds(slot * 16, 16)], fin.at[which, block], stage1_from[slot])
+            send(backp.at[which, pl.ds(slot * 16, 16)], fin.at[which, block], stage2_from[slot])
             for slot in range(1, 8)
         ]
 
@@ -463,7 +442,8 @@
     ob[0] = (
         full[0, 0:128, :].astype(F32) + gate * (ao[0:128, :] + cr[0].astype(F32))
     ).astype(BF)
-    res2 = back_stage2(0)
+    res_z = back_first(0)
+    sum_middle(1, sum_b)
     swapped[1].wait_recv()
 
     def layer_back(i, carry):
@@ -484,19 +464,18 @@
         return carry
 
     lax.fori_loop(0, 4, layer_back, 0)
-    gin2 = back_stage2(1)
+    gin_z = back_first(1)
     sum_a = z_start(0, sum_a)
-    arrived(res2)
-    res1 = back_stage1(0)
     sum_b = second_start(1, sum_b)
-    arrived(gin2)
-    gin1 = back_stage1(1)
-    sum_b = second_middle(1, sum_b)
+    arrived(res_z)
+    res_xy = back_last(0)
+    arrived(gin_z)
+    gin_xy = back_last(1)
     sum_b = z_start(1, sum_b)
-    arrived(res1)
-    res_out[...] = fin[0]
-    arrived(gin1)
-    gin_out[...] = fin[1]
+    arrived(res_xy)
+    res_out[...] = mm(swap[...], fin[0]).astype(BF)
+    arrived(gin_xy)
+    gin_out[...] = mm(swap[...], fin[1]).astype(BF)
     arrived(sum_a)
     arrived(sum_b)
     total = zb[0, rows(z * 48, 48), :].astype(F32)
@@ -510,6 +489,11 @@
         copy.wait_send()
 
 
+def place(*refs):
+    for i in range(4):
+        refs[4 + i][...] = refs[i][...]
+
+
 N_COPY = 160
 
 
@@ -529,14 +513,17 @@
             jax.ShapeDtypeStruct((18, 3, HC), F32),
             jax.ShapeDtypeStruct((18, HC), F32),
         ),
-        in_specs=[vm] * 6 + [anys] * 2 + [vm, anys] + [vm] * 5,
+        in_specs=[vm] * 8 + [anys] * 7,
         out_specs=(vm, vm, vm, vm),
         scratch_shapes=[
             vmem((D, D)),
             vmem((D, D)),
+            vmem((320, 288)),
+            vmem((320, 288)),
+            vmem((192, 80)),
+            vmem((192, 80)),
             vmem((2, D, W2)),
-            vmem((2, 128, D)),
-            vmem((2, 128, D)),
+            *[vmem((128, D))] * 6,
             vmem((2, 256, D)),
             vmem((256, D)),
             vmem((D, 256)),
@@ -563,8 +550,7 @@
             vmem((2, 2, 2, 144, W2)),
             vmem((2, 2, 6, 144, W2)),
             vmem((2, 2, 320, W2)),
-            vmem((2, 2, 2, 48, W2)),
-            vmem((2, 2, 6, 48, W2)),
+            vmem((2, 2, 3, 80, W2)),
             vmem((2, 192, W2)),
             vmem((7, 48, W2)),
             vmem((2, 128, D)),
@@ -573,7 +559,7 @@
             vmem((2, 128, D)),
             vmem((2, 128, D)),
             vmem((2, 128, D)),
-            pltpu.SemaphoreType.DMA((3,)),
+            pltpu.SemaphoreType.DMA((7,)),
             pltpu.SemaphoreType.DMA((N_COPY,)),
             pltpu.SemaphoreType.DMA((N_COPY,)),
         ],
@@ -582,10 +568,18 @@
         ),
         name="sublayer",
     )(
-        tokens_in, grad_result, mod_shift, mod_scale, branch_gate, norm_gain,
+        tokens_in, grad_result, mod_shift, mod_scale, branch_gate, norm_gain, swap, heads,
         jnp.transpose(inproj, (1, 2, 0)).reshape(3 * HC, D), outproj,
-        swap, turn, first, second, upper, lower, heads,
+        turn, first, second, upper, lower,
     )
+    made = [result, grad_in, grad_inproj, grad_outproj]
+    result, grad_in, grad_inproj, grad_outproj = pl.pallas_call(
+        place,
+        out_shape=[jax.ShapeDtypeStruct(v.shape, v.dtype) for v in made],
+        in_specs=[vm] * 4,
+        out_specs=[vm] * 4,
+        name="place",
+    )(*made)
     return result, grad_in, grad_inproj, grad_outproj.T
 
 

time: 121 us -> 107 us (0.88)
  the two profiles are of different devices: /device:TPU:1 before, /device:TPU:64 now
where the time goes in v3:
time: 107 us
  Pallas kernels  106 us (99%)
    pallas_call x1, Pallas kernels, body(): pl.pallas_call(kernel, out_shape=(jax.ShapeDtypeStruct((128, D), BF), jax...  105 us

profile of v3, /device:TPU:64, one launch (start us, length us, event | category | flops | bytes accessed | tf_op | source)
XLA Modules:
  0.0 107.1 jit_solution(15495593388824431670)
XLA Ops:
  0.6 104.5 %sublayer.1 = (bf16[128,1152]{1,0:T(8,128)(2,1)}, bf16[128,1152]{1,0:T(8,128)(2,1)}, f32[18,3,288]{2,1,0:T(4,128)}, f32[18,288]{1,0:T(8,128)}) custom-call(bf16[128,1152]{1,0:T(8,128)(2,1)} %tok.1, bf16[128,1152]{1,0:T(8,128)(2,1)} %grd.1, f32[1152]{0:T(1024)} %shift_in.1, f32[1152]{0:T(1024)} %scale_in.1, f32[1152]{0:T(1024)} %gate_in.1, f32[2,72]{1,0:T(2,128)} %gain_in.1, ...), custom_call_target="tpu_custom_call" | custom-call | tf_op jit(solution)/shard_map/sublayer/pallas_call | solution.py:508
  105.1 1.9 %place.1 = (bf16[128,1152]{1,0:T(8,128)(2,1)}, bf16[128,1152]{1,0:T(8,128)(2,1)}, f32[18,3,288]{2,1,0:T(4,128)}, f32[18,288]{1,0:T(8,128)}) custom-call(bf16[128,1152]{1,0:T(8,128)(2,1)} %get-tuple-element.12.refs_0_, bf16[128,1152]{1,0:T(8,128)(2,1)} %get-tuple-element.13.refs_1_, f32[18,3,288]{2,1,0:T(4,128)} %get-tuple-element.14.refs_2_, ...), custom_call_target="tpu_custom_call" | custom-call | tf_op jit(solution)/shard_map/place/pallas_call | solution.py:576

commit v4 on v3

--- a/solution.py
+++ b/solution.py
@@ -284,7 +284,7 @@
             acc_k[...] += mm_tn(ds, qh)
             return carry
 
-        lax.fori_loop(0, 4, head, 0, unroll=2)
+        lax.fori_loop(0, 4, head, 0, unroll=4)
 
     def unnorm(cot, raw, r, gain):
         n = raw * r
@@ -419,6 +419,7 @@
     cs[1] = gm[128:256, :].astype(BF)
     swapped = [send(cs.at[i], cr.at[i], core) for i in range(2)]
     sum_a = second_start(0, sum_a)
+    sum_middle(1, sum_b)
 
     def back_first(which):
         ob[which] = mm(swap[...], ob[which]).astype(BF)
@@ -443,7 +444,6 @@
         full[0, 0:128, :].astype(F32) + gate * (ao[0:128, :] + cr[0].astype(F32))
     ).astype(BF)
     res_z = back_first(0)
-    sum_middle(1, sum_b)
     swapped[1].wait_recv()
 
     def layer_back(i, carry):

time: 107 us -> 105 us (0.981)
  Pallas kernels: 106 us -> 104 us
    pallas_call x1, Pallas kernels: 105 us -> 102 us  [body(): pl.pallas_call(kernel, out_shape=(jax.ShapeDtypeStruct((128, D), BF), jax...]
where the time goes in v4:
time: 105 us
  Pallas kernels  104 us (99%)
    pallas_call x1, Pallas kernels, body(): pl.pallas_call(kernel, out_shape=(jax.ShapeDtypeStruct((128, D), BF), jax...  102 us

profile of v4, /device:TPU:64, one launch (start us, length us, event | category | flops | bytes accessed | tf_op | source)
XLA Modules:
  0.0 104.8 jit_solution(9867115138746455497)
XLA Ops:
  0.6 102.2 %sublayer.1 = (bf16[128,1152]{1,0:T(8,128)(2,1)}, bf16[128,1152]{1,0:T(8,128)(2,1)}, f32[18,3,288]{2,1,0:T(4,128)}, f32[18,288]{1,0:T(8,128)}) custom-call(bf16[128,1152]{1,0:T(8,128)(2,1)} %tok.1, bf16[128,1152]{1,0:T(8,128)(2,1)} %grd.1, f32[1152]{0:T(1024)} %shift_in.1, f32[1152]{0:T(1024)} %scale_in.1, f32[1152]{0:T(1024)} %gate_in.1, f32[2,72]{1,0:T(2,128)} %gain_in.1, ...), custom_call_target="tpu_custom_call" | custom-call | tf_op jit(solution)/shard_map/sublayer/pallas_call | solution.py:508
  102.8 1.9 %place.1 = (bf16[128,1152]{1,0:T(8,128)(2,1)}, bf16[128,1152]{1,0:T(8,128)(2,1)}, f32[18,3,288]{2,1,0:T(4,128)}, f32[18,288]{1,0:T(8,128)}) custom-call(bf16[128,1152]{1,0:T(8,128)(2,1)} %get-tuple-element.12.refs_0_, bf16[128,1152]{1,0:T(8,128)(2,1)} %get-tuple-element.13.refs_1_, f32[18,3,288]{2,1,0:T(4,128)} %get-tuple-element.14.refs_2_, ...), custom_call_target="tpu_custom_call" | custom-call | tf_op jit(solution)/shard_map/place/pallas_call | solution.py:576

commit v5 on v4

--- a/solution.py
+++ b/solution.py
@@ -469,9 +469,9 @@
     sum_b = second_start(1, sum_b)
     arrived(res_z)
     res_xy = back_last(0)
+    sum_b = z_start(1, sum_b)
     arrived(gin_z)
     gin_xy = back_last(1)
-    sum_b = z_start(1, sum_b)
     arrived(res_xy)
     res_out[...] = mm(swap[...], fin[0]).astype(BF)
     arrived(gin_xy)

time: 105 us -> 105 us (level)
  no operation moved by 1% of the time
where the time goes in v5:
time: 105 us; the launch traced here: 104 us
  Pallas kernels  104 us (99%)
    pallas_call x1, Pallas kernels, body(): pl.pallas_call(kernel, out_shape=(jax.ShapeDtypeStruct((128, D), BF), jax...  102 us

profile of v5, /device:TPU:64, one launch (start us, length us, event | category | flops | bytes accessed | tf_op | source)
XLA Modules:
  0.0 104.2 jit_solution(4999467694953804752)
XLA Ops:
  0.6 101.6 %sublayer.1 = (bf16[128,1152]{1,0:T(8,128)(2,1)}, bf16[128,1152]{1,0:T(8,128)(2,1)}, f32[18,3,288]{2,1,0:T(4,128)}, f32[18,288]{1,0:T(8,128)}) custom-call(bf16[128,1152]{1,0:T(8,128)(2,1)} %tok.1, bf16[128,1152]{1,0:T(8,128)(2,1)} %grd.1, f32[1152]{0:T(1024)} %shift_in.1, f32[1152]{0:T(1024)} %scale_in.1, f32[1152]{0:T(1024)} %gate_in.1, f32[2,72]{1,0:T(2,128)} %gain_in.1, ...), custom_call_target="tpu_custom_call" | custom-call | tf_op jit(solution)/shard_map/sublayer/pallas_call | solution.py:508
  102.3 1.9 %place.1 = (bf16[128,1152]{1,0:T(8,128)(2,1)}, bf16[128,1152]{1,0:T(8,128)(2,1)}, f32[18,3,288]{2,1,0:T(4,128)}, f32[18,288]{1,0:T(8,128)}) custom-call(bf16[128,1152]{1,0:T(8,128)(2,1)} %get-tuple-element.12.refs_0_, bf16[128,1152]{1,0:T(8,128)(2,1)} %get-tuple-element.13.refs_1_, f32[18,3,288]{2,1,0:T(4,128)} %get-tuple-element.14.refs_2_, ...), custom_call_target="tpu_custom_call" | custom-call | tf_op jit(solution)/shard_map/place/pallas_call | solution.py:576
